TPU v7x, 32 devices: a whole 2x2x4 slice. The times are simulated.
32 devices in a mesh: side: 2 (over x), dp: 16 (over z, y, core).
Axes of the slice: x: 2, y: 2, z: 4, core: 2. Of those that a mesh axis runs over, the one named last changes fastest.
Arguments:
- decoder_in: bfloat16 [32, 512, 768], P(('side', 'dp')), may hold values from -6 to 6
- encoder_out: bfloat16 [32, 1024, 768], P(('side', 'dp')), may hold values from -6 to 6
- segment_ids: int32 [32, 512], P(('side', 'dp')), may hold values from 0 to 7, never falling along the last dimension, each value on 1 to 256 neighbouring positions
- cotangent: float32 [32, 512, 768], P(('side', 'dp')), may hold values from -6 to 6
- attn_master: float32 [6144, 768], P(('side', 'dp'))
- ffn_master: float32 [6144, 768], P(('side', 'dp'))
- small_master: float32 [17, 768], replicated
- attn_moment: float32 [6144, 768], P(('side', 'dp')), may hold values from -384 to 384
- ffn_moment: float32 [6144, 768], P(('side', 'dp')), may hold values from -384 to 384
- small_moment: float32 [17, 768], replicated, may hold values from -384 to 384
- attn_average: float32 [6144, 768], P(('side', 'dp')), may hold values from -0.5 to 0.5
- ffn_average: float32 [6144, 768], P(('side', 'dp')), may hold values from -0.5 to 0.5
- small_average: float32 [17, 768], replicated, may hold values from -6 to 6
- rate_matrix: float32 [], replicated, may hold values from 8.457279e-05 to 0.00016914558
- rate_vector: float32 [], replicated, may hold values from 0.00078125 to 0.00234375
Outputs:
- layer_out: float32 [32, 512, 768], P(('side', 'dp'))
- input_grad: float32 [32, 512, 768], P(('side', 'dp'))
- encoder_grad: float32 [32, 1024, 768], P(('side', 'dp'))
- attn_grad: float32 [6144, 768], P(('side', 'dp'))
- ffn_grad: float32 [6144, 768], P(('side', 'dp'))
- small_grad: float32 [17, 768], replicated
- attn_new: float32 [6144, 768], P(('side', 'dp'))
- ffn_new: float32 [6144, 768], P(('side', 'dp'))
- small_new: float32 [17, 768], replicated
- attn_moment_new: float32 [6144, 768], P(('side', 'dp'))
- ffn_moment_new: float32 [6144, 768], P(('side', 'dp'))
- small_moment_new: float32 [17, 768], replicated
- attn_average_new: float32 [6144, 768], P(('side', 'dp'))
- ffn_average_new: float32 [6144, 768], P(('side', 'dp'))
- small_average_new: float32 [17, 768], replicated
Inputs may be any that keep to these rules, and one draw needn't show every extreme that they name: `segment_ids`: along each row the ids never fall; each segment holds 1 to 256 positions, one exactly 256.
All inputs are finite; a program needn't handle non-finite values.
Results may differ from a plain program's by a relative error of at most 0.024.
The roundings to bfloat16 on the way count: a program that leaves them out, or rounds other values in their place, can miss the bound.
Values may be sent and summed in bfloat16 or wider, within the bound.
A program may use at most 192 MiB of HBM per device.

v0:
```python
import math

import jax
import jax.numpy as jnp
from jax import lax
from jax.sharding import PartitionSpec as P

HEADS = 12
HEAD_DIM = 64


NEG_FILL = -1e30
EPSILON = 1e-05
MOMENTUM = 0.5
AVG_DECAY = 0.5


def partner(value, axis, apart):
    mask = 2**apart
    pairs = [(source, source ^ mask) for source in range(lax.axis_size(axis))]
    return lax.ppermute(value, axis, pairs)


def matmul(left_op, right_op):
    return jnp.dot(left_op, right_op, preferred_element_type=jnp.float32)


def contract_rows(left_op, right_op):
    return lax.dot_general(
        left_op, right_op, (((0,), (0,)), ((), ())), preferred_element_type=jnp.float32
    )


def contract_cols(left_op, right_op):
    return lax.dot_general(
        left_op, right_op, (((1,), (1,)), ((), ())), preferred_element_type=jnp.float32
    )


def gelu_exact(pre_value):
    return jax.nn.gelu(pre_value, approximate=False)


def split_heads(matrix):
    return matrix.reshape(matrix.shape[0], HEADS, HEAD_DIM)


def merge_heads(tensor):
    return tensor.reshape(tensor.shape[0], HEADS * HEAD_DIM)


def column_sum(grad_low):
    return jnp.sum(grad_low.astype(jnp.float32), axis=0)


def norm_forward(residual, norm_gain, norm_shift):
    row_mean = jnp.mean(residual, axis=-1, keepdims=True)
    centered = residual - row_mean
    row_var = jnp.mean(centered * centered, axis=-1, keepdims=True)
    inv_std = lax.rsqrt(row_var + EPSILON)
    normed = centered * inv_std
    return (normed * norm_gain + norm_shift, normed, inv_std)


def norm_backward(grad_out, normed, inv_std, norm_gain):
    grad_norm = grad_out * norm_gain
    centered_grad = grad_norm - jnp.mean(grad_norm, axis=-1, keepdims=True)
    grad_res = inv_std * (
        centered_grad - normed * jnp.mean(grad_norm * normed, axis=-1, keepdims=True)
    )
    return (grad_res, jnp.sum(grad_out * normed, axis=0), jnp.sum(grad_out, axis=0))


def block_scores(q_block, keys_in, seg_row, first_row):
    scores = jnp.einsum("qhd,khd->hqk", q_block, keys_in, preferred_element_type=jnp.float32)
    if seg_row is None:
        return scores
    block_len = q_block.shape[0]
    query_pos = first_row + jnp.arange(block_len)
    key_pos = jnp.arange(seg_row.shape[0])
    allowed = (key_pos[None, :] <= query_pos[:, None]) & (seg_row[:, None] == seg_row[None, :])
    return jnp.where(allowed[None], scores, NEG_FILL)


def attend_forward(queries, keys_in, values_in, seg_row):
    scores = block_scores(queries, keys_in, seg_row, 0)
    row_max = jnp.max(scores, axis=-1, keepdims=True)
    exp_scores = jnp.exp(scores - row_max)
    totals = jnp.sum(exp_scores, axis=-1, keepdims=True)
    attn_prob = (exp_scores / totals).astype(jnp.bfloat16)
    outputs = jnp.einsum("hqk,khd->qhd", attn_prob, values_in, preferred_element_type=jnp.float32)
    lse_list = [row_max + jnp.log(totals)]
    return (outputs, lse_list)


def attend_backward(queries, keys_in, values_in, seg_row, lse_list, grad_mixed):
    query_len = queries.shape[0]
    block_len = min(512, query_len)
    grad_queries = []
    grad_keys = jnp.zeros(keys_in.shape, jnp.float32)
    grad_values = jnp.zeros(values_in.shape, jnp.float32)
    for block_index, first_row in enumerate(range(0, query_len, block_len)):
        scores = block_scores(queries, keys_in, seg_row, first_row)
        attn_prob = jnp.exp(scores - lse_list[block_index])
        grad_values = jnp.einsum(
            "hqk,qhd->khd",
            attn_prob.astype(jnp.bfloat16),
            grad_mixed,
            preferred_element_type=jnp.float32,
        )
        grad_prob = jnp.einsum(
            "qhd,khd->hqk", grad_mixed, values_in, preferred_element_type=jnp.float32
        )
        grad_scores = attn_prob * (
            grad_prob - jnp.sum(grad_prob * attn_prob, axis=-1, keepdims=True)
        )
        grad_low = grad_scores.astype(jnp.bfloat16)
        grad_queries.append(
            jnp.einsum("hqk,khd->qhd", grad_low, keys_in, preferred_element_type=jnp.float32)
        )
        grad_keys = jnp.einsum(
            "hqk,qhd->khd", grad_low, queries, preferred_element_type=jnp.float32
        )
    grad_q_all = grad_queries[0].astype(jnp.bfloat16)
    return (grad_q_all, grad_keys.astype(jnp.bfloat16), grad_values.astype(jnp.bfloat16))


def layer_row(dec_row, enc_row, seg_row, cot_row, blocks, w_in, w_out, vectors):
    w_query, w_key, w_value, w_proj, c_query, c_key, c_value, c_proj = blocks
    scale = 1.0 / math.sqrt(HEAD_DIM)
    bias_in = vectors[13:].reshape(-1)
    dec_full = dec_row.astype(jnp.float32)
    queries = ((matmul(dec_row, w_query) + vectors[0]) * scale).astype(jnp.bfloat16)
    keys_self = matmul(dec_row, w_key).astype(jnp.bfloat16)
    vals_self = (matmul(dec_row, w_value) + vectors[1]).astype(jnp.bfloat16)
    mixed_self, lse_self = attend_forward(
        split_heads(queries), split_heads(keys_self), split_heads(vals_self), seg_row
    )
    self_flat = merge_heads(mixed_self).astype(jnp.bfloat16)
    self_out = matmul(self_flat, w_proj) + vectors[2]
    hidden_one, normed_one, inv_one = norm_forward(dec_full + self_out, vectors[7], vectors[8])
    hidden_one_low = hidden_one.astype(jnp.bfloat16)
    cross_q = ((matmul(hidden_one_low, c_query) + vectors[3]) * scale).astype(jnp.bfloat16)
    cross_k = matmul(enc_row, c_key).astype(jnp.bfloat16)
    cross_v = (matmul(enc_row, c_value) + vectors[4]).astype(jnp.bfloat16)
    mixed_cross, lse_cross = attend_forward(
        split_heads(cross_q), split_heads(cross_k), split_heads(cross_v), None
    )
    cross_flat = merge_heads(mixed_cross).astype(jnp.bfloat16)
    cross_out = matmul(cross_flat, c_proj) + vectors[5]
    hidden_two, normed_two, inv_two = norm_forward(hidden_one + cross_out, vectors[9], vectors[10])
    hidden_two_low = hidden_two.astype(jnp.bfloat16)
    pre_act = contract_cols(hidden_two_low, w_in) + bias_in
    act_full, act_pull = jax.vjp(gelu_exact, pre_act)
    act_low = act_full.astype(jnp.bfloat16)
    ffn_out = matmul(act_low, w_out) + vectors[6]
    result, normed_three, inv_three = norm_forward(hidden_two + ffn_out, vectors[11], vectors[12])
    grad_r3, grad_g3, grad_e3 = norm_backward(cot_row, normed_three, inv_three, vectors[11])
    grad_y = grad_r3.astype(jnp.bfloat16)
    grad_w_out = contract_rows(act_low, grad_y)
    grad_act = contract_cols(grad_y, w_out)
    grad_pre = act_pull(grad_act)[0].astype(jnp.bfloat16)
    grad_w_in = contract_rows(grad_pre, hidden_two_low)
    grad_h2 = grad_r3 + matmul(grad_pre, w_in)
    grad_r2, grad_g2, grad_e2 = norm_backward(grad_h2, normed_two, inv_two, vectors[9])
    grad_co = grad_r2.astype(jnp.bfloat16)
    grad_c_proj = contract_rows(cross_flat, grad_co)
    grad_mix_c = contract_cols(grad_co, c_proj).astype(jnp.bfloat16)
    grad_q_c, grad_k_c, grad_v_c = attend_backward(
        split_heads(cross_q),
        split_heads(cross_k),
        split_heads(cross_v),
        None,
        lse_cross,
        split_heads(grad_mix_c),
    )
    grad_cq = merge_heads(grad_q_c) * scale
    grad_ck = merge_heads(grad_k_c)
    grad_cv = merge_heads(grad_v_c)
    grad_c_query = contract_rows(hidden_one_low, grad_cq)
    grad_h1 = grad_r2 + contract_cols(grad_cq, c_query)
    grad_r1, grad_g1, grad_e1 = norm_backward(grad_h1, normed_one, inv_one, vectors[7])
    grad_so = grad_r1.astype(jnp.bfloat16)
    grad_w_proj = contract_rows(self_flat, grad_so)
    grad_mix_s = contract_cols(grad_so, w_proj).astype(jnp.bfloat16)
    grad_q_s, grad_k_s, grad_v_s = attend_backward(
        split_heads(queries),
        split_heads(keys_self),
        split_heads(vals_self),
        seg_row,
        lse_self,
        split_heads(grad_mix_s),
    )
    grad_sq = merge_heads(grad_q_s) * scale
    grad_sk = merge_heads(grad_k_s)
    grad_sv = merge_heads(grad_v_s)
    grad_w_query = contract_rows(dec_row, grad_sq)
    grad_w_key = contract_rows(dec_row, grad_sk)
    grad_w_value = contract_rows(dec_row, grad_sv)
    grad_input = (
        grad_r1
        + contract_cols(grad_sq, w_query)
        + contract_cols(grad_sk, w_key)
        + contract_cols(grad_sv, w_value)
    )
    vec_rows = jnp.stack(
        [
            column_sum(grad_sq),
            column_sum(grad_sv),
            column_sum(grad_so),
            column_sum(grad_cq),
            column_sum(grad_cv),
            column_sum(grad_co),
            column_sum(grad_y),
            grad_g1,
            grad_e1,
            grad_g2,
            grad_e2,
            grad_g3,
            grad_e3,
        ]
    )
    vec_grad = jnp.concatenate([vec_rows, column_sum(grad_pre).reshape(-1, vectors.shape[1])], 0)
    row_mats = (grad_w_query, grad_w_key, grad_w_value, grad_w_proj, grad_c_query, grad_c_proj)
    return (result, grad_input, grad_ck, grad_cv, row_mats, grad_w_in, grad_w_out, vec_grad)


def nesterov(master, moment, average, grad, rate):
    new_moment = MOMENTUM * moment + grad
    new_master = master - rate * (grad + MOMENTUM * new_moment)
    new_average = AVG_DECAY * average + (1.0 - AVG_DECAY) * new_master
    return (new_master, new_moment, new_average)


def local(
    decoder_in,
    encoder_out,
    segment_ids,
    cotangent,
    attn_master,
    ffn_master,
    small_master,
    attn_moment,
    ffn_moment,
    small_moment,
    attn_average,
    ffn_average,
    small_average,
    rate_matrix,
    rate_vector,
):
    matrices, ffn_all = (
        lax.all_gather(attn_master.astype(jnp.bfloat16), ("side", "dp"), axis=0, tiled=True),
        lax.all_gather(ffn_master.astype(jnp.bfloat16), ("side", "dp"), axis=0, tiled=True),
    )
    model_width = matrices.shape[1]
    hidden_units = ffn_all.shape[0] // 2
    blocks = [
        matrices[block_index * model_width : (block_index + 1) * model_width]
        for block_index in range(8)
    ]
    w_in = ffn_all[:hidden_units]
    w_out = ffn_all[hidden_units:]
    partner_enc = partner(encoder_out, "side", 0)
    mat_grads = [jnp.zeros((model_width, model_width), jnp.float32) for block_index in range(8)]
    slots = (0, 1, 2, 3, 4, 7)
    row_index = 0
    outcome = layer_row(
        decoder_in[row_index],
        partner_enc[row_index],
        segment_ids[row_index],
        cotangent[row_index],
        blocks,
        w_in,
        w_out,
        small_master,
    )
    result, grad_input, grad_ck, grad_cv, row_mats, grad_w_in, grad_w_out, vec_grad = outcome
    results = [result]
    input_grads = [grad_input]
    key_grads = [grad_ck]
    value_grads = [grad_cv]
    for slot_index, slot_grad in zip(slots, row_mats):
        mat_grads[slot_index] = slot_grad
    returned = partner(jnp.stack([jnp.stack(key_grads), jnp.stack(value_grads)]), "side", 0)
    row_index = 0
    own_rows = encoder_out[row_index]
    mat_grads[5] = contract_rows(own_rows, returned[0, row_index])
    mat_grads[6] = contract_rows(own_rows, returned[1, row_index])
    enc_grads = [
        contract_cols(returned[0, row_index], blocks[5])
        + contract_cols(returned[1, row_index], blocks[6])
    ]
    encoder_grad = jnp.stack(enc_grads)
    attn_total = jnp.concatenate(mat_grads, 0)
    ffn_total = jnp.concatenate([grad_w_in, grad_w_out], 0)
    attn_grad, ffn_grad = (
        lax.psum_scatter(attn_total, ("side", "dp"), scatter_dimension=0, tiled=True),
        lax.psum_scatter(ffn_total, ("side", "dp"), scatter_dimension=0, tiled=True),
    )
    small_grad = lax.psum(vec_grad, ("side", "dp"))
    attn_new, attn_moment_new, attn_average_new = nesterov(
        attn_master, attn_moment, attn_average, attn_grad, rate_matrix
    )
    ffn_new, ffn_moment_new, ffn_average_new = nesterov(
        ffn_master, ffn_moment, ffn_average, ffn_grad, rate_matrix
    )
    small_new, small_moment_new, small_average_new = nesterov(
        small_master, small_moment, small_average, small_grad, rate_vector
    )
    layer_out = jnp.stack(results)
    input_grad = jnp.stack(input_grads)
    return (
        layer_out,
        input_grad,
        encoder_grad,
        attn_grad,
        ffn_grad,
        small_grad,
        attn_new,
        ffn_new,
        small_new,
        attn_moment_new,
        ffn_moment_new,
        small_moment_new,
        attn_average_new,
        ffn_average_new,
        small_average_new,
    )


def solution(mesh):
    placed = (
        P(("side", "dp"), None, None),
        P(("side", "dp"), None, None),
        P(("side", "dp"), None),
        P(("side", "dp"), None, None),
        P(("side", "dp"), None),
        P(("side", "dp"), None),
        P(),
        P(("side", "dp"), None),
        P(("side", "dp"), None),
        P(),
        P(("side", "dp"), None),
        P(("side", "dp"), None),
        P(),
        P(),
        P(),
    )
    return jax.shard_map(
        local,
        mesh=mesh,
        in_specs=placed,
        out_specs=(
            P(("side", "dp"), None, None),
            P(("side", "dp"), None, None),
            P(("side", "dp"), None, None),
            P(("side", "dp"), None),
            P(("side", "dp"), None),
            P(),
            P(("side", "dp"), None),
            P(("side", "dp"), None),
            P(),
            P(("side", "dp"), None),
            P(("side", "dp"), None),
            P(),
            P(("side", "dp"), None),
            P(("side", "dp"), None),
            P(),
        ),
        check_vma=False,
    )
```

profile of v0, /device:TPU:0, one launch (start us, length us, event | category | flops | bytes accessed | tf_op | source)
XLA Modules:
  0.0 687.8 jit_solution(14238010336797911645)
XLA Ops:
  7.2 1.8 convert_element_type.152
  9.1 1.8 convert_element_type.169
  11.0 3.0 collective-permute-start
  14.8 1.3 slice_reduce_fusion.1
  17.1 88.3 %all-gather.3.cloned.1.call-done = bf16[6144,768]{1,0:T(8,128)(2,1)} async-done(((bf16[192,768]{1,0:T(8,128)(2,1)}), bf16[6144,768]{1,0:T(8,128)(2,1)}) %all-gather.3.cloned.1.call-update) | async-done | bytes 9437200 | tf_op jit(solution)/shard_map/all_gather | solution.py:253
  105.4 2.3 multiply_convert_fusion.4
  108.0 2.3 add_convert_fusion.2
  110.6 3.2 convolution_convert_fusion.4
  113.9 1.4 copy.48
  115.3 1.9 select_reduce_fusion
  117.3 2.2 fusion.6
  119.5 2.4 copy-done
  122.0 3.5 fusion.46
  125.6 2.5 fusion.94
  129.2 2.2 multiply_convert_fusion.3
  131.7 3.5 convolution_convert_fusion.1
  135.2 3.7 add_convert_fusion.1
  139.0 10.2 %fusion.95 = (f32[12,512]{1,0:T(8,128)S(1)}, f32[12,512,1024]{2,1,0:T(8,128)}) fusion(bf16[512,12,64]{0,2,1:T(8,128)(2,1)S(1)} %bitcast.136, bf16[1024,12,64]{0,2,1:T(8,128)(2,1)S(1)} %bitcast.146), kind=kOutput, calls=%fused_computation.196 | convolution fusion | flops 811591680 | bytes 27549696 | tf_op jit(solution)/shard_map/qhd,khd->hqk/dot_general | solution.py:75
  149.2 11.9 %fusion = f32[12,512]{1,0:T(8,128)S(1)} fusion(f32[12,512,1024]{2,1,0:T(8,128)} %get-tuple-element.62, f32[12,512]{1,0:T(8,128)S(1)} %get-tuple-element.61), kind=kLoop, calls=%fused_computation.5 | loop fusion | flops 12576768 | bytes 25214976 | tf_op jit(solution)/shard_map/reduce_sum | solution.py:89
  161.1 10.7 %fusion.47 = bf16[12,64,512]{2,1,0:T(8,128)(2,1)S(1)} fusion(bf16[1024,12,64]{0,2,1:T(8,128)(2,1)S(1)} %bitcast.156, f32[12,512,1024]{2,1,0:T(8,128)} %get-tuple-element.62, f32[12,512]{1,0:T(8,128)S(1)} %fusion, f32[12,512]{1,0:T(8,128)S(1)} %get-tuple-element.61), kind=kOutput, calls=%fused_computation.114 | convolution fusion | flops 824573952 | bytes 27574272 | tf_op jit(solution)/shard_map/hqk,khd->qhd/dot_general | solution.py:91
  171.8 2.7 fusion.96
  174.8 14.7 %all-gather.5.cloned.1.call-done = bf16[6144,768]{1,0:T(8,128)(2,1)} async-done(((bf16[192,768]{1,0:T(8,128)(2,1)}), bf16[6144,768]{1,0:T(8,128)(2,1)}) %all-gather.5.cloned.1.call-update) | async-done | bytes 9437200 | tf_op jit(solution)/shard_map/all_gather | solution.py:254
  189.5 21.0 %multiply_convert_fusion.2 = (bf16[512,3072]{1,0:T(8,128)(2,1)S(1)}, f32[512,3072]{1,0:T(8,128)}, f32[512,3072]{1,0:T(8,128)}) fusion(f32[3072]{0:T(1024)S(1)} %add.241, bf16[6144,768]{1,0:T(8,128)(2,1)} %all-gather.5.cloned.1.call-done, f32[512,768]{1,0:T(8,128)S(1)} %get-tuple-element.64, f32[768]{0:T(1024)S(1)} %get-tuple-element.28, ...), kind=kOutput, calls=%fused_computation.25 | convolution fusion | flops 2521694208 | bytes 22042624 | tf_op jit(solution)/shard_map/dot_general | solution.py:35
  210.6 2.8 fusion.97
  213.7 1.2 fusion.35
  214.9 2.3 convert_reduce_fusion.2
  217.2 2.7 fusion.83
  219.9 7.5 %convert_reduce_fusion = (f32[3072]{0:T(1024)S(1)}, bf16[512,3072]{1,0:T(8,128)(2,1)S(1)}) fusion(f32[512,3072]{1,0:T(8,128)} %get-tuple-element.55, bf16[6144,768]{1,0:T(8,128)(2,1)S(1)} %copy-done.56, f32[512,768]{1,0:T(8,128)S(1)} %get-tuple-element.49, f32[512,3072]{1,0:T(8,128)} %get-tuple-element.65, f32[3072]{0:T(1024)S(1)} %add.241), kind=kOutput, calls=%fused_computation.22 | convolution fusion | flops 2443047936 | bytes 22044672 | tf_op jit(solution)/shard_map/dot_general | solution.py:35
  227.5 2.8 fusion.88
  230.3 10.8 %pad_maximum_fusion = f32[6144,768]{1,0:T(8,128)} fusion(f32[3072,768]{1,0:T(8,128)S(1)} %fusion.83, f32[3072,768]{1,0:T(8,128)S(1)} %fusion.88), kind=kLoop, calls=%fused_computation.7 | loop fusion | flops 4718592 | bytes 37748736 | tf_op jit(solution)/shard_map/concatenate | solution.py:296
  241.2 6.3 multiply_reduce_fusion.2
  249.2 2.2 convolution_convert_fusion.3
  251.8 22.2 %multiply_reduce_fusion = (f32[12,512]{1,0:T(8,128)S(1)}, f32[12,512,1024]{2,1,0:T(8,128)}) fusion(f32[12,512,1024]{2,1,0:T(8,128)} %get-tuple-element.62, f32[12,512]{1,0:T(8,128)S(1)} %log_add_fusion.1, bf16[512,12,64]{0,2,1:T(8,128)(2,1)S(1)} %bitcast.141, bf16[1024,12,64]{0,2,1:T(8,128)(2,1)S(1)} %bitcast.157), kind=kOutput, calls=%fused_computation.1 | convolution fusion | flops 824174592 | bytes 52740096 | tf_op jit(solution)/shard_map/qhd,khd->hqk/dot_general | solution.py:111
  273.9 19.6 %multiply_convert_fusion = bf16[12,512,1024]{2,1,0:T(8,128)(2,1)S(1)} fusion(f32[12,512,1024]{2,1,0:T(8,128)} %get-tuple-element.70, f32[12,512,1024]{2,1,0:T(8,128)} %get-tuple-element.62, f32[12,512]{1,0:T(8,128)S(1)} %get-tuple-element.69, f32[12,512]{1,0:T(8,128)S(1)} %log_add_fusion.1), kind=kLoop, calls=%fused_computation | loop fusion | flops 25165824 | bytes 62963712 | tf_op jit(solution)/shard_map/convert_element_type | solution.py:117
  293.6 7.4 %convert_reduce_fusion.4 = (f32[12,64]{1,0:T(8,128)S(1)}, bf16[12,64,512]{2,1,0:T(8,128)(2,1)}) fusion(bf16[1024,12,64]{0,2,1:T(8,128)(2,1)} %bitcast.147, bf16[12,512,1024]{2,1,0:T(8,128)(2,1)S(1)} %multiply_convert_fusion), kind=kOutput, calls=%fused_computation.78 | convolution fusion | flops 806878464 | bytes 14945280 | tf_op jit(solution)/shard_map/hqk,khd->qhd/dot_general | solution.py:119
  301.0 4.0 multiply_reduce_fusion.3
  305.5 2.2 convolution_convert_fusion.2
  308.9 7.1 %convolution_convert_fusion = bf16[12,64,1024]{2,1,0:T(8,128)(2,1)S(1)} fusion(bf16[512,12,64]{0,2,1:T(8,128)(2,1)S(1)} %bitcast.137, bf16[12,512,1024]{2,1,0:T(8,128)(2,1)} %copy-done.1), kind=kOutput, calls=%fused_computation.62 | convolution fusion | flops 806092800 | bytes 14942208 | tf_op jit(solution)/shard_map/hqk,qhd->khd/dot_general | solution.py:121
  316.0 12.7 %convert_reduce_fusion.1 = (f32[12,64]{1,0:T(8,128)S(1)}, bf16[12,64,1024]{2,1,0:T(8,128)(2,1)}) fusion(bf16[512,12,64]{0,2,1:T(8,128)(2,1)S(1)} %bitcast.142, f32[12,512,1024]{2,1,0:T(8,128)} %get-tuple-element.62, f32[12,512]{1,0:T(8,128)S(1)} %log_add_fusion.1), kind=kOutput, calls=%fused_computation.51 | convolution fusion | flops 820247808 | bytes 27552768 | tf_op jit(solution)/shard_map/hqk,qhd->khd/dot_general | solution.py:105
  328.7 1.8 pad_maximum_fusion.1
  330.6 1.6 collective-permute-start.1
  332.3 6.6 multiply_reduce_fusion.1
  338.9 7.2 %multiply_convert_fusion.1 = bf16[12,512,512]{1,2,0:T(8,128)(2,1)S(1)} fusion(f32[12,512,512]{1,2,0:T(8,128)} %get-tuple-element.73, f32[12,512,512]{1,2,0:T(8,128)S(1)} %bitcast.133, f32[12,512]{1,0:T(8,128)S(1)} %get-tuple-element.72, f32[12,512]{1,0:T(8,128)S(1)} %log_add_fusion, pred[512,512]{0,1:T(8,128)(4,1)S(1)} %copy-done.15), kind=kLoop, calls=%fused_computation.9 | loop fusion | flops 15728640 | bytes 31768576 | tf_op jit(solution)/shard_map/convert_element_type | solution.py:117
  346.1 1.2 convert_reduce_fusion.7
  347.3 2.2 bitcast_dynamic-update-slice_fusion.4
  349.6 2.0 convolution_convert_fusion.5
  351.6 2.2 bitcast_dynamic-update-slice_fusion.3
  353.8 3.3 convert_reduce_fusion.6
  357.1 2.3 bitcast_dynamic-update-slice_fusion.2
  359.4 2.3 convolution_dynamic-update-slice_fusion.2
  361.7 2.5 convolution_dynamic-update-slice_fusion.1
  364.2 62.2 %collective-permute-done.1 = bf16[2,1,1024,768]{2,3,1,0:T(8,128)(2,1)} collective-permute-done((bf16[2,1,1024,768]{2,3,1,0:T(8,128)(2,1)S(1)}, bf16[2,1,1024,768]{2,3,1,0:T(8,128)(2,1)}, u32[]{:S(2)}, u32[]{:S(2)}) %collective-permute-start.1) | collective-permute-done | bytes 3145760 | tf_op jit(solution)/shard_map/ppermute | solution.py:21
  426.4 4.4 bitcast_dynamic-update-slice_fusion.1
  430.8 4.4 bitcast_dynamic-update-slice_fusion
  435.2 2.2 convolution_dynamic-update-slice_fusion
  439.7 41.9 %psum.7 = f32[17,768]{1,0:T(8,128)S(1)} all-reduce(f32[17,768]{1,0:T(8,128)S(1)} %concatenate.11), channel_id=1, replica_groups=mesh['side'=2,'dp'=16] {'side','dp'}, use_global_device_ids=true, to_apply=%region_34.35 | all-reduce | flops 13056 | bytes 104448 | tf_op jit(solution)/shard_map/psum | solution.py:301
  482.9 2.6 fusion.68
  485.5 2.2 fusion.65
  487.7 3.4 add_bitcast_fusion.1
  491.0 3.4 fusion.51
  494.5 5.2 add_bitcast_fusion
  499.8 2.6 add_multiply_fusion
  502.4 176.2 %reduce-scatter.3.cloned.1.call-done = f32[192,768]{1,0:T(8,128)} async-done(((f32[6144,768]{1,0:T(8,128)}), f32[192,768]{1,0:T(8,128)}) %reduce-scatter.3.cloned.1.call-update) | async-done | bytes 589840 | tf_op jit(solution)/shard_map/reduce_scatter | solution.py:298
  678.6 2.4 add_multiply_fusion.1
  (177 shorter events, 10.7 us)
Async XLA Ops:
  7.2 98.2 %all-gather.3.cloned.1.call-start = ((), (), s32[]{:S(2)}) async-start(), calls=%async_computation.2 | async-start | bytes 9732096 | tf_op jit(solution)/shard_map/all_gather | solution.py:253
  9.1 180.5 %all-gather.5.cloned.1.call-start = ((), (), s32[]{:S(2)}) async-start(), calls=%async_computation.3 | async-start | bytes 9732096 | tf_op jit(solution)/shard_map/all_gather | solution.py:254
  10.9 488.8 %reduce-scatter.5.cloned.1.call-start = ((), (), s32[]{:S(2)}) async-start(), calls=%async_computation.5 | async-start | bytes 19464192 | tf_op jit(solution)/shard_map/reduce_scatter | solution.py:299
  11.0 120.7 %collective-permute-start = (bf16[1,1024,768]{2,1,0:T(8,128)(2,1)}, bf16[1,1024,768]{2,1,0:T(8,128)(2,1)}, u32[]{:S(2)}, u32[]{:S(2)}) collective-permute-start(bf16[1,1024,768]{2,1,0:T(8,128)(2,1)} %param.16), channel_id=1, source_target_pairs={{0,16},{16,0},{1,17},{17,1},{2,18},{18,2},{3,19},{19,3},{4,20},{20... | collective-permute-start | bytes 4718600 | tf_op jit(solution)/shard_map/ppermute | solution.py:21
  16.1 155.7 %copy-start.54 = (f32[768]{0:T(1024)}, f32[768]{0:T(1024)S(1)}, u32[]{:S(2)}) copy-start(f32[768]{0:T(1024)S(1)} %get-tuple-element.33) | copy-start | bytes 9220
  16.1 91.9 %copy-start.12 = (bf16[1,512,768]{2,1,0:T(8,128)(2,1)S(1)}, bf16[1,512,768]{2,1,0:T(8,128)(2,1)}, u32[]{:S(2)}) copy-start(bf16[1,512,768]{2,1,0:T(8,128)(2,1)} %param.15) | copy-start | bytes 2359300
  17.1 102.4 %copy-start.14 = (pred[512,512]{0,1:T(8,128)(4,1)}, pred[512,512]{0,1:T(8,128)(4,1)S(1)}, u32[]{:S(2)}) copy-start(pred[512,512]{0,1:T(8,128)(4,1)S(1)} %fusion.54) | copy-start | bytes 786436
  108.0 7.3 %copy-start.8 = (bf16[512,768]{0,1:T(8,128)(2,1)}, bf16[512,768]{0,1:T(8,128)(2,1)S(1)}, u32[]{:S(2)}) copy-start(bf16[512,768]{0,1:T(8,128)(2,1)S(1)} %copy.47) | copy-start | bytes 2359300
  110.6 8.8 %copy-start.24 = (bf16[512,768]{0,1:T(8,128)(2,1)}, bf16[512,768]{0,1:T(8,128)(2,1)S(1)}, u32[]{:S(2)}) copy-start(bf16[512,768]{0,1:T(8,128)(2,1)S(1)} %copy.46) | copy-start | bytes 2359300
  115.3 2.0 copy-start.4
  117.2 4.6 copy-start
  117.2 4.7 copy-start.44
  119.5 6.1 copy-start.48
  125.6 2.8 copy-start.36
  131.7 7.3 %copy-start.6 = (bf16[512,768]{0,1:T(8,128)(2,1)}, bf16[512,768]{0,1:T(8,128)(2,1)S(1)}, u32[]{:S(2)}) copy-start(bf16[512,768]{0,1:T(8,128)(2,1)S(1)} %copy.50) | copy-start | bytes 2359300
  135.2 3.8 copy-start.23
  139.0 22.1 %copy-start.33 = (bf16[1024,768]{0,1:T(8,128)(2,1)}, bf16[1024,768]{0,1:T(8,128)(2,1)S(1)}, u32[]{:S(2)}) copy-start(bf16[1024,768]{0,1:T(8,128)(2,1)S(1)} %add_convert_fusion.1) | copy-start | bytes 4718596
  161.1 10.7 %copy-start.18 = (f32[512,768]{1,0:T(8,128)S(1)}, f32[512,768]{1,0:T(8,128)}, u32[]{:S(2)}) copy-start(f32[512,768]{1,0:T(8,128)} %copy-done.17) | copy-start | bytes 4718596
  171.8 2.7 copy-start.38
  189.5 21.0 %copy-start.56 = (bf16[6144,768]{1,0:T(8,128)(2,1)S(1)}, bf16[6144,768]{1,0:T(8,128)(2,1)}, u32[]{:S(2)}) copy-start(bf16[6144,768]{1,0:T(8,128)(2,1)} %all-gather.5.cloned.1.call-done) | copy-start | bytes 28311556
  210.6 3.1 copy-start.2
  227.5 2.8 copy-start.58
  241.2 437.4 %reduce-scatter.3.cloned.1.call-start = ((), (), s32[]{:S(2)}) async-start(), calls=%async_computation.4 | async-start | bytes 19464192 | tf_op jit(solution)/shard_map/reduce_scatter | solution.py:298
  248.1 3.7 copy-start.34
  251.7 22.2 %copy-start.10 = (bf16[512,768]{0,1:T(8,128)(2,1)}, bf16[512,768]{0,1:T(8,128)(2,1)S(1)}, u32[]{:S(2)}) copy-start(bf16[512,768]{0,1:T(8,128)(2,1)S(1)} %copy.51) | copy-start | bytes 2359300
  293.5 7.4 %copy-start.1 = (bf16[12,512,1024]{2,1,0:T(8,128)(2,1)}, bf16[12,512,1024]{2,1,0:T(8,128)(2,1)S(1)}, u32[]{:S(2)}) copy-start(bf16[12,512,1024]{2,1,0:T(8,128)(2,1)S(1)} %multiply_convert_fusion) | copy-start | bytes 37748740
  301.0 4.0 copy-start.19
  305.5 3.4 copy-start.7
  308.9 7.1 %copy-start.11 = (bf16[512,768]{0,1:T(8,128)(2,1)S(1)}, bf16[512,768]{0,1:T(8,128)(2,1)}, u32[]{:S(2)}) copy-start(bf16[512,768]{0,1:T(8,128)(2,1)} %copy-done.10) | copy-start | bytes 2359300
  308.9 23.4 %slice-start = ((s8[12582912]{0:T(1024)(128)(4,1)}), s8[4194304]{0:T(1024)(128)(4,1)S(1)}, s32[]{:S(2)}) async-start(s8[12582912]{0:T(1024)(128)(4,1)} %bitcast.132), calls=%async_computation.6 | async-start | bytes 8388608
  308.9 23.4 %slice-start.1 = ((s8[12582912]{0:T(1024)(128)(4,1)}), s8[4194304]{0:T(1024)(128)(4,1)S(1)}, s32[]{:S(2)}) async-start(s8[12582912]{0:T(1024)(128)(4,1)} %bitcast.132), calls=%async_computation.7 | async-start | bytes 8388608
  316.0 16.2 %slice-start.2 = ((s8[12582912]{0:T(1024)(128)(4,1)}), s8[4194304]{0:T(1024)(128)(4,1)S(1)}, s32[]{:S(2)}) async-start(s8[12582912]{0:T(1024)(128)(4,1)} %bitcast.132), calls=%async_computation.8 | async-start | bytes 8388608
  328.7 3.5 copy-start.45
  328.7 3.5 copy-start.49
  328.7 3.5 copy-start.15
  328.7 3.5 copy-start.25
  328.7 3.5 copy-start.26
  330.6 95.8 %collective-permute-start.1 = (bf16[2,1,1024,768]{2,3,1,0:T(8,128)(2,1)S(1)}, bf16[2,1,1024,768]{2,3,1,0:T(8,128)(2,1)}, u32[]{:S(2)}, u32[]{:S(2)}) collective-permute-start(bf16[2,1,1024,768]{2,3,1,0:T(8,128)(2,1)S(1)} %pad_maximum_fusion.1), channel_id=1, source_target_pairs={{0,16},{16,0},{1,17},{17,1},{2,18},{18,2},{3,19},{19,3},{4,20},{20... | collective-permute-start | bytes 9437192 | tf_op jit(solution)/shard_map/ppermute | solution.py:21
  338.9 7.2 %copy-start.5 = (bf16[512,768]{0,1:T(8,128)(2,1)S(1)}, bf16[512,768]{0,1:T(8,128)(2,1)}, u32[]{:S(2)}) copy-start(bf16[512,768]{0,1:T(8,128)(2,1)} %copy-done.4) | copy-start | bytes 2359300
  347.3 4.3 copy-start.16
  347.3 2.3 copy-start.9
  351.6 5.5 copy-start.27
  357.1 4.6 copy-start.29
  357.1 2.3 copy-start.37
  359.4 2.3 copy-start.20
  359.4 2.3 copy-start.35
  359.4 2.3 copy-start.55
  361.7 64.7 %copy-start.57 = (bf16[1,1024,768]{2,1,0:T(8,128)(2,1)S(1)}, bf16[1,1024,768]{2,1,0:T(8,128)(2,1)}, u32[]{:S(2)}) copy-start(bf16[1,1024,768]{2,1,0:T(8,128)(2,1)} %param.16) | copy-start | bytes 4718596
  430.8 4.4 copy-start.22
  430.8 4.4 copy-start.39
  437.4 1.5 copy-start.3
  437.4 1.6 copy-start.52
  437.4 1.7 copy-start.53
  437.4 44.8 %copy-start.47 = (f32[17,768]{1,0:T(8,128)S(1)}, f32[17,768]{1,0:T(8,128)}, u32[]{:S(2)}) copy-start(f32[17,768]{1,0:T(8,128)} %param.21) | copy-start | bytes 156676
  437.4 44.8 %copy-start.50 = (f32[17,768]{1,0:T(8,128)S(1)}, f32[17,768]{1,0:T(8,128)}, u32[]{:S(2)}) copy-start(f32[17,768]{1,0:T(8,128)} %param.27) | copy-start | bytes 156676
  437.4 44.8 %copy-start.51 = (f32[17,768]{1,0:T(8,128)S(1)}, f32[17,768]{1,0:T(8,128)}, u32[]{:S(2)}) copy-start(f32[17,768]{1,0:T(8,128)} %param.24) | copy-start | bytes 156676
  439.0 46.4 %copy-start.28 = (bf16[12,64,512]{2,1,0:T(8,128)(2,1)S(1)}, bf16[12,64,512]{2,1,0:T(8,128)(2,1)}, u32[]{:S(2)}) copy-start(bf16[12,64,512]{2,1,0:T(8,128)(2,1)} %copy-done.27) | copy-start | bytes 2359300
  482.9 4.8 copy-start.30
  494.5 5.3 copy-start.31
  494.5 5.3 copy-start.40
  494.5 5.3 copy-start.41
  499.7 178.8 %copy-start.32 = (f32[192,768]{1,0:T(8,128)S(1)}, f32[192,768]{1,0:T(8,128)}, u32[]{:S(2)}) copy-start(f32[192,768]{1,0:T(8,128)} %param.19) | copy-start | bytes 1769476
  499.8 178.8 %copy-start.42 = (f32[192,768]{1,0:T(8,128)S(1)}, f32[192,768]{1,0:T(8,128)}, u32[]{:S(2)}) copy-start(f32[192,768]{1,0:T(8,128)} %param.25) | copy-start | bytes 1769476
  499.8 178.8 %copy-start.43 = (f32[192,768]{1,0:T(8,128)S(1)}, f32[192,768]{1,0:T(8,128)}, u32[]{:S(2)}) copy-start(f32[192,768]{1,0:T(8,128)} %param.22) | copy-start | bytes 1769476
  (4 other events, 4.1 us)
Sparse Core Ops, SparseCore 0:
  11.5 93.8 all-gather.2
  108.9 80.6 all-gather.4
  241.3 225.9 reduce-scatter.4
  474.2 204.3 reduce-scatter.2
where the time goes:
time: 694 us; the launch traced here: 688 us
  waiting for transfers between devices  341 us (49%)
  matrix products  202 us (29%)
  other arithmetic  69.4 us (10%)
  blocking collectives  41.9 us (6%)
  between operations  16.5 us (2%)
  local copies, waits for them, and re-layouts  11.7 us (2%)
    reduce_scatter x1, waiting for transfers between devices, local(): lax.psum_scatter(attn_total, ('side', 'dp'), scatter_dimension=0, tiled=T...  176 us
    all_gather x1, waiting for transfers between devices, local(): lax.all_gather(attn_master.astype(jnp.bfloat16), ('side', 'dp'), axis=0,...  88.3 us
    ppermute x2, waiting for transfers between devices, partner(): return lax.ppermute(value, axis, pairs)  62.2 us
    dot_general x10, matrix products, contract_cols(): lax.dot_general(left_op, right_op, (((1,), (1,)), ((), ())), preferred_el...  53.7 us
    psum x1, blocking collectives, local(): small_grad = lax.psum(vec_grad, ('side', 'dp'))  41.9 us
    dot_general x10, matrix products, matmul(): return jnp.dot(left_op, right_op, preferred_element_type=jnp.float32)  31.5 us
    dot_general x2, matrix products, attend_backward(): jnp.einsum('qhd,khd->hqk', grad_mixed, values_in, preferred_element_type=...  28.8 us
    dot_general x10, matrix products, contract_rows(): lax.dot_general(left_op, right_op, (((0,), (0,)), ((), ())), preferred_el...  28.1 us
  transfers between devices with their start and end apart: 6, of which 4 were waited for; matrix products, arithmetic and copies ran while one was open for 32% of the time, Pallas kernels for 0%

commit v1 on v0

--- a/solution.py
+++ b/solution.py
@@ -1,8 +1,11 @@
+import functools
 import math
 
 import jax
 import jax.numpy as jnp
 from jax import lax
+from jax.experimental import pallas as pl
+from jax.experimental.pallas import tpu as pltpu
 from jax.sharding import PartitionSpec as P
 
 HEADS = 12
@@ -13,6 +16,423 @@
 EPSILON = 1e-05
 MOMENTUM = 0.5
 AVG_DECAY = 0.5
+
+
+MESH_ID = pl.DeviceIdType.MESH
+BF = jnp.bfloat16
+F32 = jnp.float32
+CUT = 512
+
+
+class Net:
+    def __init__(self, send_sems, recv_sems):
+        self.s = lax.axis_index("side")
+        self.d = lax.axis_index("dp")
+        self.z, self.y, self.c = self.d // 4, (self.d // 2) % 2, self.d % 2
+        self.depth = lax.axis_size("dp") // 4
+        self.send_sems, self.recv_sems = send_sems, recv_sems
+        self.sent, self.slots, self.conds = [], {}, []
+        self.low = [self.z >= k for k in range(self.depth)]
+        self.high = [self.z < self.depth - k for k in range(self.depth)]
+        self.here = [self.z == k for k in range(self.depth)]
+        self.away = [self.s != k for k in (0, 1)]
+        self.home = [self.s == k for k in (0, 1)]
+
+    def at(self, s=None, z=None, y=None, c=None):
+        s, z, y, c = (own if got is None else got for got, own in ((s, self.s), (z, self.z), (y, self.y), (c, self.c)))
+        return (s, (z * 2 + y) * 2 + c)
+
+    def slot(self, key):
+        return self.slots.setdefault(key, len(self.slots))
+
+    def copy(self, src, dst, to, send_slot, recv_slot):
+        return pltpu.make_async_remote_copy(
+            src_ref=src,
+            dst_ref=dst,
+            send_sem=self.send_sems.at[send_slot],
+            recv_sem=self.recv_sems.at[recv_slot],
+            device_id=to,
+            device_id_type=MESH_ID,
+        )
+
+    def send(self, src, dst, to, key, like):
+        send_slot, recv_slot = len(self.sent), self.slot(key)
+        self.copy(src, dst, to, send_slot, recv_slot).start()
+        peer = (self.s, self.d)
+        self.sent.append((lambda: self.copy(like(), like(), peer, send_slot, recv_slot).wait_send(), tuple(self.conds)))
+
+    def recv(self, dst, key):
+        self.copy(dst, dst, self.at(c=1 - self.c), 0, self.slot(key)).wait_recv()
+
+    def when(self, cond, body):
+        self.conds.append(cond)
+        pl.when(cond)(body)
+        self.conds.pop()
+
+    def drain(self):
+        assert max(len(self.sent), len(self.slots)) <= min(self.send_sems.shape[0], self.recv_sems.shape[0])
+        for wait, conds in self.sent:
+            for cond in conds:
+                wait = functools.partial(pl.when(cond), wait)
+            wait()
+
+    def greet(self, others=()):
+        barrier = pltpu.get_barrier_semaphore()
+        partners = [self.at(s=1 - self.s), self.at(y=1 - self.y), self.at(c=1 - self.c), *others]
+        for to in partners:
+            pl.semaphore_signal(barrier, inc=1, device_id=to, device_id_type=MESH_ID)
+        low, high = self.low[1], self.high[1]
+
+        def signal(to):
+            pl.semaphore_signal(barrier, inc=1, device_id=to, device_id_type=MESH_ID)
+
+        pl.when(low)(lambda: signal(self.at(z=self.z - 1)))
+        pl.when(high)(lambda: signal(self.at(z=self.z + 1)))
+        pl.semaphore_wait(barrier, len(partners) + low.astype(jnp.int32) + high.astype(jnp.int32))
+
+
+def gather_ticks(net, full, own, tag, placed):
+    depth, width = net.depth, full.shape[-1]
+    cols = {"A": pl.ds(0, CUT), "B": pl.ds(CUT, width - CUT)}
+    coord = {"A": (net.s, net.y), "B": (net.y, net.s)}
+    z, c = net.z, net.c
+
+    def part(p, f, z_of, l, core):
+        s, y = (f, l) if p == "A" else (l, f)
+        return full.at[s, z_of, y, core, :, cols[p]]
+
+    def pair(p, z_of, l, core):
+        if p == "A":
+            return full.at[:, z_of, l, core, :, cols[p]]
+        return full.at[l, z_of, :, core, :, cols[p]]
+
+    def dev(p, f, z_of, l, core):
+        s, y = (f, l) if p == "A" else (l, f)
+        return net.at(s, z_of, y, core)
+
+    def spread(p, src, dst, ups, rel, f_rel):
+        f, l = coord[p]
+        like = lambda: full.at[0, 0, 0, 0, :, cols[p]]
+        if ups != "down" and 1 - rel < depth:
+            net.when(
+                net.high[1],
+                lambda: net.send(src, dst, dev(p, f, z + 1, l, c), (tag, p, "up", 1 - rel, f_rel), like),
+            )
+        if ups != "up" and 1 + rel < depth:
+            net.when(
+                net.low[1],
+                lambda: net.send(src, dst, dev(p, f, z - 1, l, c), (tag, p, "down", 1 + rel, f_rel), like),
+            )
+        net.send(src, dst, dev(p, f, z, 1 - l, c), (tag, p, "l", rel, f_rel), like)
+
+    def to_core(p, rel, l_rel):
+        f, l = coord[p]
+        l_of = l if l_rel == 0 else 1 - l
+        both_f = pair(p, z + rel, l_of, c)
+        net.send(both_f, both_f, net.at(c=1 - c), (tag, p, "core", rel, l_rel), lambda: pair(p, 0, 0, 0))
+
+    def first(p):
+        f, l = coord[p]
+        src, dst = own.at[:, cols[p]], part(p, f, z, l, c)
+        net.send(src, dst, dev(p, 1 - f, z, l, c), (tag, p, "f"), lambda: full.at[0, 0, 0, 0, :, cols[p]])
+        spread(p, src, dst, "both", 0, 0)
+
+    def second(p):
+        f, l = coord[p]
+        got = part(p, 1 - f, z, l, c)
+        net.recv(got, (tag, p, "f"))
+        spread(p, got, got, "both", 0, 1)
+        to_core(p, 0, 0)
+
+    def along(p, dist, f_rel, way):
+        f, l = coord[p]
+        rel = -dist if way == "up" else dist
+
+        def body():
+            got = part(p, f if f_rel == 0 else 1 - f, z + rel, l, c)
+            net.recv(got, (tag, p, way, dist, f_rel))
+            spread(p, got, got, way, rel, f_rel)
+            if f_rel == 1:
+                to_core(p, rel, 0)
+
+        net.when(net.low[dist] if way == "up" else net.high[dist], body)
+
+    def across(p, rel):
+        f, l = coord[p]
+
+        def body():
+            for f_rel in (0, 1):
+                net.recv(part(p, f if f_rel == 0 else 1 - f, z + rel, 1 - l, c), (tag, p, "l", rel, f_rel))
+            to_core(p, rel, 1)
+
+        if rel == 0:
+            body()
+        else:
+            net.when(net.low[-rel] if rel < 0 else net.high[rel], body)
+
+    def from_core(p, rel, l_rel):
+        f, l = coord[p]
+        body = lambda: net.recv(pair(p, z + rel, l if l_rel == 0 else 1 - l, 1 - c), (tag, p, "core", rel, l_rel))
+        if rel == 0:
+            body()
+        else:
+            net.when(net.low[-rel] if rel < 0 else net.high[rel], body)
+
+    def both(fn, *args):
+        return lambda: (fn("B", *args), fn("A", *args))
+
+    ticks = [both(first), lambda: (placed(), second("B"), second("A"))]
+    for dist in range(1, depth):
+        for f_rel in (0, 1):
+            ticks.append(lambda dist=dist, f_rel=f_rel: [along(p, dist, f_rel, way) for p in "BA" for way in ("up", "down")])
+    for dist in range(depth):
+        ticks.append(lambda dist=dist: [across(p, rel) for p in "BA" for rel in sorted({-dist, dist})])
+    ticks.append(lambda: [from_core(p, rel, l_rel) for l_rel in (0, 1) for p in "BA" for rel in range(1 - depth, depth)])
+    return ticks
+
+
+def reduce_buffers(depth, rows, width):
+    half, rest = rows // 2, width - CUT
+    return {
+        "rc": (depth, 2, 2, half, width),
+        "ya": (depth, 2, half, CUT),
+        "xb": (depth, 2, half, rest),
+        "da": (depth, 2, half, CUT),
+        "ua": (depth, 2, half, CUT),
+        "db": (depth, 2, half, rest),
+        "ub": (depth, 2, half, rest),
+        "xa": (2, half, CUT),
+        "yb": (half, rest),
+        "xc": (half, rest),
+    }
+
+
+def reduce_ticks(net, part, buf, out, side, tag):
+    depth = net.depth
+    s, z, y, c = net.s, net.z, net.y, net.c
+    rc = buf["rc"]
+    a_cols, b_cols = pl.ds(0, CUT), pl.ds(CUT, rc.shape[-1] - CUT)
+    x_dev, y_dev, c_dev = net.at(s=1 - s), net.at(y=1 - y), net.at(c=1 - c)
+
+    def start(z1):
+        net.send(part.at[z1, :, 1 - c], rc.at[z1], c_dev, (tag, "c", z1), lambda: rc.at[z1])
+
+    def cores(z1):
+        net.recv(rc.at[z1], (tag, "c", z1))
+        for y1 in (0, 1):
+            rc[z1, y1] = rc[z1, y1] + part[z1, y1, c]
+        net.send(rc.at[z1, 1 - y, :, :, a_cols], buf["ya"].at[z1], y_dev, (tag, "ya", z1), lambda: buf["ya"].at[z1])
+        net.send(rc.at[z1, :, 1 - s, :, b_cols], buf["xb"].at[z1], x_dev, (tag, "xb", z1), lambda: buf["xb"].at[z1])
+
+    def add_a(z1, ref):
+        rc[z1, y, :, :, a_cols] = rc[z1, y, :, :, a_cols] + ref[...]
+
+    def add_b(z1, ref):
+        for y1 in (0, 1):
+            rc[z1, y1, s, :, b_cols] = rc[z1, y1, s, :, b_cols] + ref[y1]
+
+    def planes(z1):
+        net.recv(buf["ya"].at[z1], (tag, "ya", z1))
+        add_a(z1, buf["ya"].at[z1])
+        net.recv(buf["xb"].at[z1], (tag, "xb", z1))
+        add_b(z1, buf["xb"].at[z1])
+
+    def wave(k):
+        def go(way, z_here, order):
+            na, nb, step = ("da", "db", 1) if way == "up" else ("ua", "ub", -1)
+            for z1 in order:
+                if k > 0:
+                    net.recv(buf[na].at[z1], (tag, na, z1))
+                    add_a(z1, buf[na].at[z1])
+                    net.recv(buf[nb].at[z1], (tag, nb, z1))
+                    add_b(z1, buf[nb].at[z1])
+                if z1 != z_here:
+                    to = net.at(z=z + step)
+                    a_like, b_like = (lambda z1=z1: buf[na].at[z1]), (lambda z1=z1: buf[nb].at[z1])
+                    net.send(rc.at[z1, y, :, :, a_cols], a_like(), to, (tag, na, z1), a_like)
+                    net.send(rc.at[z1, :, s, :, b_cols], b_like(), to, (tag, nb, z1), b_like)
+
+        net.when(net.here[k], lambda: go("up", k, range(depth - 1, k - 1, -1)))
+        net.when(net.here[depth - 1 - k], lambda: go("down", depth - 1 - k, range(0, depth - k)))
+
+    def last_one():
+        net.send(rc.at[z, 1 - y, s, :, b_cols], buf["yb"], y_dev, (tag, "yb"), lambda: buf["yb"])
+        net.when(
+            net.away[side],
+            lambda: net.send(rc.at[z, y, :, :, a_cols], buf["xa"], x_dev, (tag, "xa"), lambda: buf["xa"]),
+        )
+
+    def last_two():
+        net.recv(buf["yb"], (tag, "yb"))
+        rc[z, y, s, :, b_cols] = rc[z, y, s, :, b_cols] + buf["yb"][...]
+        net.when(
+            net.away[side],
+            lambda: net.send(rc.at[z, y, s, :, b_cols], buf["xc"], x_dev, (tag, "xc"), lambda: buf["xc"]),
+        )
+
+    def last_three():
+        def body():
+            net.recv(buf["xa"], (tag, "xa"))
+            out[:, :, a_cols] = rc[z, y, :, :, a_cols].astype(F32) + buf["xa"][...].astype(F32)
+            out[s, :, b_cols] = rc[z, y, s, :, b_cols].astype(F32)
+            net.recv(buf["xc"], (tag, "xc"))
+            out[1 - s, :, b_cols] = buf["xc"][...].astype(F32)
+
+        net.when(net.home[side], body)
+
+    each = range(depth)
+    return (
+        [functools.partial(start, z1) for z1 in each],
+        [functools.partial(cores, z1) for z1 in each],
+        [functools.partial(planes, z1) for z1 in each],
+        [functools.partial(wave, k) for k in each] + [last_one, last_two, last_three],
+    )
+
+
+def flip_bit(index, bit):
+    return index + bit * (1 - 2 * ((index // bit) % 2))
+
+
+def total_partners(net):
+    bits = [2**k for k in range(net_bits(lax.axis_size("dp")))]
+    return [(net.s, flip_bit(net.d, bit)) for bit in bits] + [(1 - net.s, net.d)]
+
+
+def net_bits(number):
+    return number.bit_length() - 1
+
+
+def total_ticks(net, sums, got, tag):
+    partners = total_partners(net)
+
+    def start(k):
+        net.send(sums.at[k], got.at[k], partners[k], (tag, k), lambda: got.at[k])
+
+    def finish(k):
+        net.recv(got.at[k], (tag, k))
+        sums[k + 1] = sums[k] + got[k]
+        if k + 1 < len(partners):
+            start(k + 1)
+
+    return [functools.partial(start, 0)] + [functools.partial(finish, k) for k in range(len(partners))]
+
+
+def gather_kernel(attn_own, ffn_own, enc, attn_full, ffn_full, enc_got, send_sems, recv_sems, local_sems):
+    net = Net(send_sems, recv_sems)
+    s, z, y, c = net.s, net.z, net.y, net.c
+    net.greet()
+    moves = [
+        pltpu.make_async_copy(own, full.at[s, z, y, c], local_sems.at[k])
+        for k, (own, full) in enumerate(((attn_own, attn_full), (ffn_own, ffn_full)))
+    ]
+    for move in moves:
+        move.start()
+    attn = gather_ticks(net, attn_full, attn_own, "attn", moves[0].wait)
+    ffn = gather_ticks(net, ffn_full, ffn_own, "ffn", moves[1].wait)
+    quarter = enc.shape[0] // 4
+    attn[0]()
+    ffn[0]()
+    for k in range(4):
+        rows = pl.ds(k * quarter, quarter)
+        net.send(enc.at[rows], enc_got.at[rows], net.at(s=1 - s), ("enc", k), lambda rows=rows: enc_got.at[rows])
+    for one, two in zip(attn[1:], ffn[1:]):
+        one()
+        two()
+    for k in range(4):
+        net.recv(enc_got.at[pl.ds(k * quarter, quarter)], ("enc", k))
+    net.drain()
+
+
+def gather_call(attn_own, ffn_own, enc):
+    rows, width = attn_own.shape
+    depth = lax.axis_size("dp") // 4
+    full = jax.ShapeDtypeStruct((2, depth, 2, 2, rows, width), BF)
+    anywhere = pl.BlockSpec(memory_space=pl.ANY)
+    inside = pl.BlockSpec(memory_space=pltpu.VMEM)
+    return pl.pallas_call(
+        gather_kernel,
+        out_shape=(full, full, jax.ShapeDtypeStruct(enc.shape, enc.dtype)),
+        in_specs=[inside, inside, anywhere],
+        out_specs=(anywhere, anywhere, anywhere),
+        scratch_shapes=[
+            pltpu.SemaphoreType.DMA((192,)),
+            pltpu.SemaphoreType.DMA((192,)),
+            pltpu.SemaphoreType.DMA((2,)),
+        ],
+        compiler_params=pltpu.CompilerParams(collective_id=0, has_side_effects=True),
+        name="gather_all",
+    )(attn_own, ffn_own, enc)
+
+
+NAMES = ("rc", "ya", "xb", "da", "ua", "db", "ub", "xa", "yb", "xc")
+
+
+def reduce_kernel(attn_part, ffn_part, small, attn_out, ffn_out, small_out, send_sems, recv_sems, sums, got, *bufs):
+    net = Net(send_sems, recv_sems)
+    net.greet([to for to in total_partners(net)[2:-1]])
+    count = len(NAMES)
+    plans = []
+    for k, (part, out, side) in enumerate(((ffn_part, ffn_out, 1), (ffn_part, ffn_out, 0), (attn_part, attn_out, 1), (attn_part, attn_out, 0))):
+        buf = dict(zip(NAMES, bufs[k * count : (k + 1) * count]))
+        plans.append(reduce_ticks(net, part.at[side], buf, out, side, k))
+    sums[0] = small[...]
+    total = total_ticks(net, sums, got, "small")
+    for plan in plans:
+        for tick in plan[0]:
+            tick()
+    for plan in plans:
+        for tick in plan[1]:
+            tick()
+    total[0]()
+    total = total[1:]
+    count = len(plans)
+    for t in range(count + 1):
+        if t < count:
+            for tick in plans[t][2]:
+                tick()
+            plans[t][3][0]()
+            plans[t][3][1]()
+        if t > 0:
+            plans[t - 1][3][2]()
+            for tick in plans[t - 1][3][3:-3]:
+                tick()
+            plans[t - 1][3][-3]()
+        if t < len(total):
+            total[t]()
+        if t > 0:
+            plans[t - 1][3][-2]()
+            plans[t - 1][3][-1]()
+    for tick in total[count + 1:]:
+        tick()
+    small_out[...] = sums[sums.shape[0] - 1]
+    net.drain()
+
+
+def reduce_call(attn_part, ffn_part, small):
+    width = attn_part.shape[-1]
+    devices = lax.axis_size("dp") * 2
+    depth = lax.axis_size("dp") // 4
+    rows = attn_part.shape[0] // devices
+    shape = (2, depth, 2, 2, 2, rows // 2, width)
+    inside = pl.BlockSpec(memory_space=pltpu.VMEM)
+    shapes = reduce_buffers(depth, rows, width)
+    steps = net_bits(devices)
+    out = jax.ShapeDtypeStruct((2, rows // 2, width), F32)
+    return pl.pallas_call(
+        reduce_kernel,
+        out_shape=(out, out, jax.ShapeDtypeStruct(small.shape, F32)),
+        in_specs=[inside] * 3,
+        out_specs=(inside,) * 3,
+        scratch_shapes=[
+            pltpu.SemaphoreType.DMA((192,)),
+            pltpu.SemaphoreType.DMA((192,)),
+            pltpu.VMEM((steps + 1, *small.shape), F32),
+            pltpu.VMEM((steps, *small.shape), F32),
+            *[pltpu.VMEM(shapes[name], BF) for k in range(4) for name in NAMES],
+        ],
+        compiler_params=pltpu.CompilerParams(collective_id=1, has_side_effects=True, vmem_limit_bytes=60 << 20),
+        name="reduce_all",
+    )(attn_part.reshape(shape), ffn_part.reshape(shape), small)
 
 
 def partner(value, axis, apart):
@@ -249,10 +669,17 @@
     rate_matrix,
     rate_vector,
 ):
-    matrices, ffn_all = (
-        lax.all_gather(attn_master.astype(jnp.bfloat16), ("side", "dp"), axis=0, tiled=True),
-        lax.all_gather(ffn_master.astype(jnp.bfloat16), ("side", "dp"), axis=0, tiled=True),
-    )
+    own_kernels = attn_master.shape[0] % 32 == 0 and lax.axis_size("dp") % 4 == 0
+    attn_own, ffn_own = attn_master.astype(BF), ffn_master.astype(BF)
+    if own_kernels:
+        attn_full, ffn_full, enc_got = gather_call(attn_own, ffn_own, encoder_out[0])
+        matrices, ffn_all = (full.reshape(-1, attn_own.shape[-1]) for full in (attn_full, ffn_full))
+        partner_enc = enc_got[None]
+    else:
+        matrices, ffn_all = (
+            lax.all_gather(own, ("side", "dp"), axis=0, tiled=True) for own in (attn_own, ffn_own)
+        )
+        partner_enc = partner(encoder_out, "side", 0)
     model_width = matrices.shape[1]
     hidden_units = ffn_all.shape[0] // 2
     blocks = [
@@ -261,7 +688,6 @@
     ]
     w_in = ffn_all[:hidden_units]
     w_out = ffn_all[hidden_units:]
-    partner_enc = partner(encoder_out, "side", 0)
     mat_grads = [jnp.zeros((model_width, model_width), jnp.float32) for block_index in range(8)]
     slots = (0, 1, 2, 3, 4, 7)
     row_index = 0
@@ -282,23 +708,25 @@
     value_grads = [grad_cv]
     for slot_index, slot_grad in zip(slots, row_mats):
         mat_grads[slot_index] = slot_grad
-    returned = partner(jnp.stack([jnp.stack(key_grads), jnp.stack(value_grads)]), "side", 0)
-    row_index = 0
-    own_rows = encoder_out[row_index]
-    mat_grads[5] = contract_rows(own_rows, returned[0, row_index])
-    mat_grads[6] = contract_rows(own_rows, returned[1, row_index])
-    enc_grads = [
-        contract_cols(returned[0, row_index], blocks[5])
-        + contract_cols(returned[1, row_index], blocks[6])
-    ]
-    encoder_grad = jnp.stack(enc_grads)
-    attn_total = jnp.concatenate(mat_grads, 0)
-    ffn_total = jnp.concatenate([grad_w_in, grad_w_out], 0)
-    attn_grad, ffn_grad = (
-        lax.psum_scatter(attn_total, ("side", "dp"), scatter_dimension=0, tiled=True),
-        lax.psum_scatter(ffn_total, ("side", "dp"), scatter_dimension=0, tiled=True),
-    )
-    small_grad = lax.psum(vec_grad, ("side", "dp"))
+    mat_grads[5] = contract_rows(partner_enc[0], key_grads[0])
+    mat_grads[6] = contract_rows(partner_enc[0], value_grads[0])
+    enc_term = contract_cols(key_grads[0], blocks[5]) + contract_cols(value_grads[0], blocks[6])
+    encoder_grad = partner(enc_term.astype(BF)[None], "side", 0).astype(F32)
+    if own_kernels:
+        attn_part = jnp.concatenate([grad.astype(BF) for grad in mat_grads], 0)
+        ffn_part = jnp.concatenate([grad_w_in.astype(BF), grad_w_out.astype(BF)], 0)
+        padded = jnp.pad(vec_grad, ((0, -vec_grad.shape[0] % 8), (0, 0)))
+        attn_grad, ffn_grad, small_grad = reduce_call(attn_part, ffn_part, padded)
+        attn_grad, ffn_grad = attn_grad.reshape(attn_master.shape), ffn_grad.reshape(ffn_master.shape)
+        small_grad = small_grad[: vec_grad.shape[0]]
+    else:
+        attn_total = jnp.concatenate(mat_grads, 0)
+        ffn_total = jnp.concatenate([grad_w_in, grad_w_out], 0)
+        attn_grad, ffn_grad = (
+            lax.psum_scatter(total, ("side", "dp"), scatter_dimension=0, tiled=True)
+            for total in (attn_total, ffn_total)
+        )
+        small_grad = lax.psum(vec_grad, ("side", "dp"))
     attn_new, attn_moment_new, attn_average_new = nesterov(
         attn_master, attn_moment, attn_average, attn_grad, rate_matrix
     )

time: 694 us -> 552 us (0.80)
  waiting for transfers between devices: 341 us -> 0.01 us
  Pallas kernels: 0 us -> 259 us
  blocking collectives: 41.9 us -> 0 us
  between operations: 16.5 us -> 3.52 us
  matrix products: 202 us -> 191 us
  local copies, waits for them, and re-layouts: 11.7 us -> 21 us
    pallas_call x0 -> x2, Pallas kernels: none -> 259 us  [the longest x1 165 us: reduce_call(): pl.pallas_call(reduce_kernel, out_shape=(out, out, jax.ShapeDtypeStruct(s...]
    reduce_scatter x2 -> x0, waiting for transfers between devices: 176 us -> none  [the longest x1 176 us: local(): lax.psum_scatter(attn_total, ('side', 'dp'), scatter_dimension=0, tiled=T...]
    all_gather x2 -> x0, waiting for transfers between devices: 103 us -> none  [the longest x1 88.3 us: local(): lax.all_gather(attn_master.astype(jnp.bfloat16), ('side', 'dp'), axis=0,...]
    ppermute x2 -> x1, waiting for transfers between devices: 62.2 us -> 0.01 us  [partner(): return lax.ppermute(value, axis, pairs)]
    psum x1 -> x0, blocking collectives: 41.9 us -> none  [local(): small_grad = lax.psum(vec_grad, ('side', 'dp'))]
    slice x0 -> x1, local copies, waits for them, and re-layouts: none -> 8.47 us  [local(): w_out = ffn_all[hidden_units:]]
  transfers between devices with their start and end apart: 6 -> 1, of which waited for: 4 -> 0; matrix products, arithmetic and copies ran while one was open for 32% -> 17% of each run, Pallas kernels for 0% -> 31%
where the time goes in v1:
time: 552 us; the launch traced here: 541 us
  Pallas kernels  259 us (47%)
  matrix products  191 us (35%)
  other arithmetic  64.6 us (12%)
  local copies, waits for them, and re-layouts  21 us (4%)
    pallas_call x1, Pallas kernels, reduce_call(): pl.pallas_call(reduce_kernel, out_shape=(out, out, jax.ShapeDtypeStruct(s...  165 us
    pallas_call x1, Pallas kernels, gather_call(): pl.pallas_call(gather_kernel, out_shape=(full, full, jax.ShapeDtypeStruct...  93.9 us
    dot_general x10, matrix products, contract_cols(): lax.dot_general(left_op, right_op, (((1,), (1,)), ((), ())), preferred_el...  53.2 us
    dot_general x2, matrix products, attend_backward(): jnp.einsum('qhd,khd->hqk', grad_mixed, values_in, preferred_element_type=...  31 us
    dot_general x10, matrix products, matmul(): return jnp.dot(left_op, right_op, preferred_element_type=jnp.float32)  28 us
    dot_general x10, matrix products, contract_rows(): lax.dot_general(left_op, right_op, (((0,), (0,)), ((), ())), preferred_el...  25.7 us
    convert_element_type x2, other arithmetic, attend_backward(): grad_low = grad_scores.astype(jnp.bfloat16)  24.5 us
    dot_general x2, matrix products, attend_forward(): jnp.einsum('hqk,khd->qhd', attn_prob, values_in, preferred_element_type=j...  14.1 us
  transfers between devices with their start and end apart: 1, of which 0 were waited for; matrix products, arithmetic and copies ran while one was open for 17% of the time, Pallas kernels for 31%

profile of v1, /device:TPU:0, one launch (start us, length us, event | category | flops | bytes accessed | tf_op | source)
XLA Modules:
  0.0 541.3 jit_solution(17845865473432803464)
XLA Ops:
  0.6 1.2 slice_reduce_fusion.1
  2.7 1.8 convert_element_type.208.attn_own
  4.5 1.8 convert_element_type.209.ffn_own
  6.3 93.9 %gather_all.1 = (bf16[2,4,2,2,192,768]{5,4,3,2,1,0:T(8,128)(2,1)}, bf16[2,4,2,2,192,768]{5,4,3,2,1,0:T(8,128)(2,1)}, bf16[1024,768]{1,0:T(8,128)(2,1)}) custom-call(bf16[192,768]{1,0:T(8,128)(2,1)} %convert_element_type.208.attn_own, bf16[192,768]{1,0:T(8,128)(2,1)} %convert_element_type.209.ffn_own, bf16[1024,768]{1,0:T(8,128)(2,1)} %bitcast.177), custom_call_target="tpu_custom_call" | custom-call | tf_op jit(solution)/shard_map/gather_all/pallas_call | solution.py:352
  100.2 8.5 %fusion.89 = (bf16[1,4,2,2,192,768]{5,4,3,2,1,0:T(8,128)(2,1)}, bf16[1,4,2,2,192,768]{5,4,3,2,1,0:T(8,128)(2,1)}) fusion(bf16[2,4,2,2,192,768]{5,4,3,2,1,0:T(8,128)(2,1)} %get-tuple-element.23), kind=kLoop, calls=%fused_computation.194 | loop fusion | bytes 18874368 | tf_op jit(solution)/shard_map/slice | solution.py:690
  108.7 3.9 convolution_convert_fusion.3
  112.6 3.9 add_convert_fusion.2
  116.5 2.1 convolution_convert_fusion.14
  118.6 2.4 add_convert_fusion.3
  121.3 2.2 multiply_convert_fusion.4
  123.5 2.0 select_reduce_fusion
  125.5 2.2 fusion.6
  127.8 2.2 copy-done
  130.3 3.7 fusion.39
  134.0 2.5 fusion.90
  136.8 2.4 multiply_convert_fusion.3
  139.5 11.8 %fusion.91 = (f32[12,512]{1,0:T(8,128)S(1)}, f32[12,512,1024]{2,1,0:T(8,128)}) fusion(bf16[512,12,64]{0,2,1:T(8,128)(2,1)S(1)} %bitcast.147, bf16[1024,12,64]{0,2,1:T(8,128)(2,1)} %bitcast.153), kind=kOutput, calls=%fused_computation.196 | convolution fusion | flops 811591680 | bytes 27549696 | tf_op jit(solution)/shard_map/qhd,khd->hqk/dot_general | solution.py:495
  151.4 11.6 %fusion = f32[12,512]{1,0:T(8,128)S(1)} fusion(f32[12,512,1024]{2,1,0:T(8,128)} %get-tuple-element.77, f32[12,512]{1,0:T(8,128)S(1)} %get-tuple-element.76), kind=kLoop, calls=%fused_computation.5 | loop fusion | flops 12576768 | bytes 25214976 | tf_op jit(solution)/shard_map/reduce_sum | solution.py:509
  163.0 10.5 %fusion.40 = bf16[12,64,512]{2,1,0:T(8,128)(2,1)S(1)} fusion(bf16[1024,12,64]{0,2,1:T(8,128)(2,1)S(1)} %bitcast.173, f32[12,512,1024]{2,1,0:T(8,128)} %get-tuple-element.77, f32[12,512]{1,0:T(8,128)S(1)} %fusion, f32[12,512]{1,0:T(8,128)S(1)} %get-tuple-element.76), kind=kOutput, calls=%fused_computation.113 | convolution fusion | flops 824573952 | bytes 27574272 | tf_op jit(solution)/shard_map/hqk,khd->qhd/dot_general | solution.py:511
  173.5 2.6 fusion.92
  176.6 19.6 %multiply_convert_fusion.2 = (bf16[512,3072]{1,0:T(8,128)(2,1)S(1)}, f32[512,3072]{1,0:T(8,128)}, f32[512,3072]{1,0:T(8,128)}) fusion(f32[3072]{0:T(1024)S(1)} %add.239, bf16[3072,768]{1,0:T(8,128)(2,1)S(1)} %bitcast.157, f32[512,768]{1,0:T(8,128)S(1)} %get-tuple-element.79, f32[768]{0:T(1024)S(1)} %get-tuple-element.40, f32[768]{0:T(1024)S(1)} %get-tuple-element.41, ...), kind=kOutput, calls=%fused_computation.25 | convolution fusion | flops 2521694208 | bytes 22042624 | tf_op jit(solution)/shard_map/dot_general | solution.py:455
  196.2 2.8 fusion.93
  200.1 1.8 convert_reduce_fusion.2
  201.9 8.4 %convert_reduce_fusion = (f32[3072]{0:T(1024)S(1)}, bf16[512,3072]{1,0:T(8,128)(2,1)S(1)}) fusion(f32[512,3072]{1,0:T(8,128)} %get-tuple-element.68, bf16[3072,768]{1,0:T(8,128)(2,1)S(1)} %bitcast.162, f32[512,768]{1,0:T(8,128)S(1)} %get-tuple-element.62, f32[512,3072]{1,0:T(8,128)} %get-tuple-element.80, f32[3072]{0:T(1024)S(1)} %add.239), kind=kOutput, calls=%fused_computation.22 | convolution fusion | flops 2443047936 | bytes 22044672 | tf_op jit(solution)/shard_map/dot_general | solution.py:455
  210.3 3.1 multiply_reduce_fusion.2
  214.0 1.2 copy-done.9
  215.2 2.1 convolution_convert_fusion.13
  217.6 19.7 %multiply_reduce_fusion = (f32[12,512]{1,0:T(8,128)S(1)}, f32[12,512,1024]{2,1,0:T(8,128)}) fusion(f32[12,512,1024]{2,1,0:T(8,128)} %get-tuple-element.77, f32[12,512]{1,0:T(8,128)S(1)} %log_add_fusion.1, bf16[512,12,64]{0,2,1:T(8,128)(2,1)S(1)} %bitcast.149, bf16[1024,12,64]{0,2,1:T(8,128)(2,1)S(1)} %bitcast.174), kind=kOutput, calls=%fused_computation.1 | convolution fusion | flops 824174592 | bytes 52740096 | tf_op jit(solution)/shard_map/qhd,khd->hqk/dot_general | solution.py:531
  237.2 10.6 %convert_reduce_fusion.1 = (f32[12,64]{1,0:T(8,128)S(1)}, bf16[12,64,1024]{2,1,0:T(8,128)(2,1)S(1)}) fusion(bf16[512,12,64]{0,2,1:T(8,128)(2,1)S(1)} %bitcast.150, f32[12,512,1024]{2,1,0:T(8,128)} %get-tuple-element.77, f32[12,512]{1,0:T(8,128)S(1)} %log_add_fusion.1), kind=kOutput, calls=%fused_computation.44 | convolution fusion | flops 820247808 | bytes 27552768 | tf_op jit(solution)/shard_map/hqk,qhd->khd/dot_general | solution.py:525
  247.8 17.5 %multiply_convert_fusion = bf16[12,512,1024]{2,1,0:T(8,128)(2,1)S(1)} fusion(f32[12,512,1024]{2,1,0:T(8,128)} %get-tuple-element.85, f32[12,512,1024]{2,1,0:T(8,128)} %get-tuple-element.77, f32[12,512]{1,0:T(8,128)S(1)} %get-tuple-element.84, f32[12,512]{1,0:T(8,128)S(1)} %log_add_fusion.1), kind=kLoop, calls=%fused_computation | loop fusion | flops 25165824 | bytes 62963712 | tf_op jit(solution)/shard_map/convert_element_type | solution.py:537
  265.4 2.3 convolution_convert_fusion.2
  267.7 3.3 fusion.49
  271.1 4.0 fusion.29
  275.0 1.5 collective-permute-start
  276.6 6.2 %convert_reduce_fusion.4 = (f32[12,64]{1,0:T(8,128)S(1)}, bf16[12,64,512]{2,1,0:T(8,128)(2,1)}) fusion(bf16[1024,12,64]{0,2,1:T(8,128)(2,1)} %bitcast.154, bf16[12,512,1024]{2,1,0:T(8,128)(2,1)S(1)} %multiply_convert_fusion), kind=kOutput, calls=%fused_computation.57 | convolution fusion | flops 806878464 | bytes 14945280 | tf_op jit(solution)/shard_map/hqk,khd->qhd/dot_general | solution.py:539
  282.8 4.0 multiply_reduce_fusion.3
  287.4 3.0 convolution_convert_fusion.12
  290.4 1.4 copy.43
  291.8 11.4 %multiply_reduce_fusion.1 = (f32[12,512]{1,0:T(8,128)S(1)}, f32[12,512,512]{1,2,0:T(8,128)}) fusion(f32[12,512,512]{1,2,0:T(8,128)} %copy-done, f32[12,512]{1,0:T(8,128)S(1)} %log_add_fusion, pred[512,512]{0,1:T(8,128)(4,1)S(1)} %copy-done.6, bf16[512,12,64]{0,2,1:T(8,128)(2,1)S(1)} %bitcast.163, bf16[512,12,64]{0,2,1:T(8,128)(2,1)} %bitcast.179), kind=kOutput, calls=%fused_computation.9 | convolution fusion | flops 415229952 | bytes 27049984 | tf_op jit(solution)/shard_map/qhd,khd->hqk/dot_general | solution.py:531
  303.2 1.7 slice-done.2
  304.9 7.0 %multiply_convert_fusion.1 = bf16[12,512,512]{1,2,0:T(8,128)(2,1)S(1)} fusion(f32[12,512,512]{1,2,0:T(8,128)} %get-tuple-element.88, f32[12,512,512]{1,2,0:T(8,128)S(1)} %bitcast.145, f32[12,512]{1,0:T(8,128)S(1)} %get-tuple-element.87, f32[12,512]{1,0:T(8,128)S(1)} %log_add_fusion, pred[512,512]{0,1:T(8,128)(4,1)S(1)} %copy-done.6), kind=kLoop, calls=%fused_computation.8 | loop fusion | flops 15728640 | bytes 31768576 | tf_op jit(solution)/shard_map/convert_element_type | solution.py:537
  312.0 2.0 convolution_convert_fusion.15
  314.0 1.2 convert_reduce_fusion.7
  315.2 3.1 convert_reduce_fusion.6
  318.4 4.4 convolution_convert_fusion
  322.8 4.9 convolution_convert_fusion.1
  327.7 3.3 fusion.58
  331.0 1.8 fusion.31
  332.9 1.9 fusion.33
  334.7 1.9 fusion.35
  336.6 1.8 fusion.28
  338.5 2.1 fusion.27
  340.6 2.5 fusion.26
  343.1 2.5 fusion.25
  345.6 1.9 fusion.24
  348.8 8.8 %pad_maximum_fusion = bf16[6144,768]{1,0:T(8,128)(2,1)} fusion(bf16[3072,768]{1,0:T(8,128)(2,1)} %convolution_convert_fusion, bf16[3072,768]{1,0:T(8,128)(2,1)} %convolution_convert_fusion.1), kind=kLoop, calls=%fused_computation.18 | loop fusion | flops 18874368 | bytes 18874368 | tf_op jit(solution)/shard_map/concatenate | solution.py:717
  357.6 165.5 %reduce_all.1 = (f32[2,96,768]{2,1,0:T(8,128)}, f32[2,96,768]{2,1,0:T(8,128)}, f32[24,768]{1,0:T(8,128)}) custom-call(bf16[2,4,2,2,2,96,768]{6,5,4,3,2,1,0:T(8,128)(2,1)} %bitcast.51.attn_part, bf16[2,4,2,2,2,96,768]{6,5,4,3,2,1,0:T(8,128)(2,1)} %bitcast.146, f32[24,768]{1,0:T(8,128)} %pad.4.small), custom_call_target="tpu_custom_call" | custom-call | tf_op jit(solution)/shard_map/reduce_all/pallas_call | solution.py:421
  524.5 1.7 add_multiply_fusion.2
  526.2 2.2 fusion.61
  528.5 2.7 add_multiply_fusion.1
  531.3 1.3 add_multiply_fusion
  532.6 3.3 add_bitcast_fusion
  535.9 3.3 convert_element_type.251
  539.2 0.8 copy.62
  (183 shorter events, 7.0 us)
Async XLA Ops:
  1.9 171.6 %copy-start.53 = (f32[768]{0:T(1024)}, f32[768]{0:T(1024)S(1)}, u32[]{:S(2)}) copy-start(f32[768]{0:T(1024)S(1)} %get-tuple-element.45) | copy-start | bytes 9220
  100.2 8.5 %copy-start.55 = (bf16[1024,768]{1,0:T(8,128)(2,1)S(1)}, bf16[1024,768]{1,0:T(8,128)(2,1)}, u32[]{:S(2)}) copy-start(bf16[1024,768]{1,0:T(8,128)(2,1)} %get-tuple-element.22) | copy-start | bytes 4718596
  112.6 3.9 copy-start.57
  118.6 4.9 copy-start.7
  118.6 2.4 copy-start.52
  121.0 6.7 %copy-start.35 = (bf16[768,512]{1,0:T(8,128)(2,1)}, bf16[768,512]{1,0:T(8,128)(2,1)S(1)}, u32[]{:S(2)}) copy-start(bf16[768,512]{1,0:T(8,128)(2,1)S(1)} %add_convert_fusion.3) | copy-start | bytes 2359300
  121.3 6.5 %copy-start.5 = (pred[512,512]{0,1:T(8,128)(4,1)}, pred[512,512]{0,1:T(8,128)(4,1)S(1)}, u32[]{:S(2)}) copy-start(pred[512,512]{0,1:T(8,128)(4,1)S(1)} %fusion.46) | copy-start | bytes 786436
  125.5 4.5 copy-start
  125.5 4.7 copy-start.45
  127.7 6.2 %copy-start.48 = (f32[12,512]{1,0:T(8,128)}, f32[12,512]{1,0:T(8,128)S(1)}, u32[]{:S(2)}) copy-start(f32[12,512]{1,0:T(8,128)S(1)} %fusion.6) | copy-start | bytes 73732
  134.0 2.8 copy-start.37
  136.5 37.0 %copy-start.11 = (f32[512,768]{1,0:T(8,128)}, f32[512,768]{1,0:T(8,128)S(1)}, u32[]{:S(2)}) copy-start(f32[512,768]{1,0:T(8,128)S(1)} %get-tuple-element.75) | copy-start | bytes 4718596
  139.5 11.9 %copy-start.3 = (bf16[512,768]{0,1:T(8,128)(2,1)}, bf16[512,768]{0,1:T(8,128)(2,1)S(1)}, u32[]{:S(2)}) copy-start(bf16[512,768]{0,1:T(8,128)(2,1)S(1)} %copy.41) | copy-start | bytes 2359300
  151.4 11.7 %copy-start.28 = (bf16[1024,768]{0,1:T(8,128)(2,1)S(1)}, bf16[1024,768]{0,1:T(8,128)(2,1)}, u32[]{:S(2)}) copy-start(bf16[1024,768]{0,1:T(8,128)(2,1)} %add_convert_fusion.2) | copy-start | bytes 4718596
  151.4 25.2 %slice-start.3 = ((s8[4718592]{0:T(1024)(128)(4,1)}), s8[4194304]{0:T(1024)(128)(4,1)S(1)}, s32[]{:S(2)}) async-start(s8[4718592]{0:T(1024)(128)(4,1)} %bitcast.155), calls=%async_computation.3 | async-start | bytes 8388608
  163.0 13.5 %slice-start.4 = ((s8[4718592]{0:T(1024)(128)(4,1)}), s8[524288]{0:T(1024)(128)(4,1)S(1)}, s32[]{:S(2)}) async-start(s8[4718592]{0:T(1024)(128)(4,1)} %bitcast.155), calls=%async_computation.4 | async-start | bytes 1048576
  173.5 2.7 copy-start.39
  173.5 22.7 %slice-start.5 = ((s8[4718592]{0:T(1024)(128)(4,1)}), s8[4194304]{0:T(1024)(128)(4,1)S(1)}, s32[]{:S(2)}) async-start(s8[4718592]{0:T(1024)(128)(4,1)} %bitcast.159), calls=%async_computation.5 | async-start | bytes 8388608
  176.2 37.3 %copy-start.14 = (f32[512,768]{1,0:T(8,128)}, f32[512,768]{1,0:T(8,128)S(1)}, u32[]{:S(2)}) copy-start(f32[512,768]{1,0:T(8,128)S(1)} %get-tuple-element.79) | copy-start | bytes 4718596
  176.6 19.6 %slice-start.6 = ((s8[4718592]{0:T(1024)(128)(4,1)}), s8[524288]{0:T(1024)(128)(4,1)S(1)}, s32[]{:S(2)}) async-start(s8[4718592]{0:T(1024)(128)(4,1)} %bitcast.159), calls=%async_computation.6 | async-start | bytes 1048576
  196.2 2.9 copy-start.59
  196.2 3.2 copy-start.1
  201.9 8.4 %copy-start.32 = (f32[512,768]{1,0:T(8,128)}, f32[512,768]{1,0:T(8,128)S(1)}, u32[]{:S(2)}) copy-start(f32[512,768]{1,0:T(8,128)S(1)} %get-tuple-element.62) | copy-start | bytes 4718596
  210.3 3.1 copy-start.61
  214.0 3.6 copy-start.29
  247.8 23.2 %copy-start.30 = (bf16[12,64,1024]{2,1,0:T(8,128)(2,1)}, bf16[12,64,1024]{2,1,0:T(8,128)(2,1)S(1)}, u32[]{:S(2)}) copy-start(bf16[12,64,1024]{2,1,0:T(8,128)(2,1)S(1)} %get-tuple-element.96) | copy-start | bytes 4718596
  247.8 17.5 %copy-start.4 = (bf16[512,768]{0,1:T(8,128)(2,1)S(1)}, bf16[512,768]{0,1:T(8,128)(2,1)}, u32[]{:S(2)}) copy-start(bf16[512,768]{0,1:T(8,128)(2,1)} %copy-done.3) | copy-start | bytes 2359300
  267.7 3.3 copy-start.20
  271.1 5.5 %copy-start.46 = (f32[12,512]{1,0:T(8,128)S(1)}, f32[12,512]{1,0:T(8,128)}, u32[]{:S(2)}) copy-start(f32[12,512]{1,0:T(8,128)} %copy-done.45) | copy-start | bytes 73732
  271.1 5.5 %copy-start.49 = (f32[12,512]{1,0:T(8,128)S(1)}, f32[12,512]{1,0:T(8,128)}, u32[]{:S(2)}) copy-start(f32[12,512]{1,0:T(8,128)} %copy-done.48) | copy-start | bytes 73732
  275.0 260.9 %collective-permute-start = (bf16[1,1024,768]{2,1,0:T(8,128)(2,1)}, bf16[1,1024,768]{2,1,0:T(8,128)(2,1)}, u32[]{:S(2)}, u32[]{:S(2)}) collective-permute-start(bf16[1,1024,768]{2,1,0:T(8,128)(2,1)} %fusion.29), channel_id=1, source_target_pairs={{0,16},{16,0},{1,17},{17,1},{2,18},{18,2},{3,19},{19,3},{4,20},{20... | collective-permute-start | bytes 4718600 | tf_op jit(solution)/shard_map/ppermute | solution.py:441
  282.8 4.0 copy-start.12
  287.3 4.5 copy-start.6
  291.8 11.4 %copy-start.16 = (bf16[512,768]{0,1:T(8,128)(2,1)}, bf16[512,768]{0,1:T(8,128)(2,1)S(1)}, u32[]{:S(2)}) copy-start(bf16[512,768]{0,1:T(8,128)(2,1)S(1)} %copy.43) | copy-start | bytes 2359300
  291.8 11.4 %slice-start = ((s8[12582912]{0:T(1024)(128)(4,1)}), s8[4194304]{0:T(1024)(128)(4,1)S(1)}, s32[]{:S(2)}) async-start(s8[12582912]{0:T(1024)(128)(4,1)} %bitcast.144), calls=%async_computation | async-start | bytes 8388608
  291.8 11.4 %slice-start.1 = ((s8[12582912]{0:T(1024)(128)(4,1)}), s8[4194304]{0:T(1024)(128)(4,1)S(1)}, s32[]{:S(2)}) async-start(s8[12582912]{0:T(1024)(128)(4,1)} %bitcast.144), calls=%async_computation.1 | async-start | bytes 8388608
  291.8 13.1 %slice-start.2 = ((s8[12582912]{0:T(1024)(128)(4,1)}), s8[4194304]{0:T(1024)(128)(4,1)S(1)}, s32[]{:S(2)}) async-start(s8[12582912]{0:T(1024)(128)(4,1)} %bitcast.144), calls=%async_computation.2 | async-start | bytes 8388608
  304.9 7.0 %copy-start.19 = (bf16[768,512]{1,0:T(8,128)(2,1)S(1)}, bf16[768,512]{1,0:T(8,128)(2,1)}, u32[]{:S(2)}) copy-start(bf16[768,512]{1,0:T(8,128)(2,1)} %copy-done.18) | copy-start | bytes 2359300
  315.2 15.8 %copy-start.22 = (bf16[12,64,512]{2,1,0:T(8,128)(2,1)}, bf16[12,64,512]{2,1,0:T(8,128)(2,1)S(1)}, u32[]{:S(2)}) copy-start(bf16[12,64,512]{2,1,0:T(8,128)(2,1)S(1)} %get-tuple-element.90) | copy-start | bytes 2359300
  315.2 3.1 copy-start.33
  315.2 3.1 copy-start.60
  318.3 16.4 %copy-start.41 = (bf16[12,64,512]{2,1,0:T(8,128)(2,1)}, bf16[12,64,512]{2,1,0:T(8,128)(2,1)S(1)}, u32[]{:S(2)}) copy-start(bf16[12,64,512]{2,1,0:T(8,128)(2,1)S(1)} %get-tuple-element.92) | copy-start | bytes 2359300
  318.4 4.4 copy-start.15
  318.4 4.4 copy-start.62
  327.7 3.3 copy-start.58
  332.9 3.8 copy-start.38
  334.7 3.8 copy-start.13
  334.7 3.8 copy-start.36
  334.7 3.8 copy-start.54
  340.6 2.5 copy-start.31
  343.1 2.5 copy-start.10
  343.1 2.5 copy-start.40
  357.6 166.9 %copy-start.47 = (f32[17,768]{1,0:T(8,128)S(1)}, f32[17,768]{1,0:T(8,128)}, u32[]{:S(2)}) copy-start(f32[17,768]{1,0:T(8,128)} %param.21) | copy-start | bytes 156676
  357.6 166.9 %copy-start.50 = (f32[17,768]{1,0:T(8,128)S(1)}, f32[17,768]{1,0:T(8,128)}, u32[]{:S(2)}) copy-start(f32[17,768]{1,0:T(8,128)} %param.27) | copy-start | bytes 156676
  357.6 166.9 %copy-start.51 = (f32[17,768]{1,0:T(8,128)S(1)}, f32[17,768]{1,0:T(8,128)}, u32[]{:S(2)}) copy-start(f32[17,768]{1,0:T(8,128)} %param.24) | copy-start | bytes 156676
  357.6 168.5 %copy-start.23 = (bf16[12,64,512]{2,1,0:T(8,128)(2,1)S(1)}, bf16[12,64,512]{2,1,0:T(8,128)(2,1)}, u32[]{:S(2)}) copy-start(bf16[12,64,512]{2,1,0:T(8,128)(2,1)} %copy-done.22) | copy-start | bytes 2359300
  523.1 5.4 copy-start.24
  524.5 4.0 copy-start.27
  526.2 5.1 copy-start.25
  526.2 5.1 copy-start.26
  526.2 5.1 copy-start.43
  526.2 5.1 copy-start.44
  528.5 4.1 copy-start.34
  528.5 4.1 copy-start.42
  (7 other events, 12.9 us)

commit v2 on v1

--- a/solution.py
+++ b/solution.py
@@ -22,6 +22,12 @@
 BF = jnp.bfloat16
 F32 = jnp.float32
 CUT = 512
+
+
+def run_when(cond, body):
+    @pl.when(cond)
+    def _():
+        body()
 
 
 class Net:
@@ -66,7 +72,7 @@
 
     def when(self, cond, body):
         self.conds.append(cond)
-        pl.when(cond)(body)
+        run_when(cond, body)
         self.conds.pop()
 
     def drain(self):
@@ -91,7 +97,7 @@
         pl.semaphore_wait(barrier, len(partners) + low.astype(jnp.int32) + high.astype(jnp.int32))
 
 
-def gather_ticks(net, full, own, tag, placed):
+def gather_ticks(net, full, own, tag):
     depth, width = net.depth, full.shape[-1]
     cols = {"A": pl.ds(0, CUT), "B": pl.ds(CUT, width - CUT)}
     coord = {"A": (net.s, net.y), "B": (net.y, net.s)}
@@ -181,7 +187,7 @@
     def both(fn, *args):
         return lambda: (fn("B", *args), fn("A", *args))
 
-    ticks = [both(first), lambda: (placed(), second("B"), second("A"))]
+    ticks = [both(first), both(second)]
     for dist in range(1, depth):
         for f_rel in (0, 1):
             ticks.append(lambda dist=dist, f_rel=f_rel: [along(p, dist, f_rel, way) for p in "BA" for way in ("up", "down")])
@@ -197,17 +203,15 @@
         "rc": (depth, 2, 2, half, width),
         "ya": (depth, 2, half, CUT),
         "xb": (depth, 2, half, rest),
-        "da": (depth, 2, half, CUT),
-        "ua": (depth, 2, half, CUT),
-        "db": (depth, 2, half, rest),
-        "ub": (depth, 2, half, rest),
+        "za": (depth + 1, 2, half, CUT),
+        "zb": (depth + 1, 2, half, rest),
         "xa": (2, half, CUT),
         "yb": (half, rest),
         "xc": (half, rest),
     }
 
 
-def reduce_ticks(net, part, buf, out, side, tag):
+def reduce_ticks(net, part, own, buf, out, side, tag):
     depth = net.depth
     s, z, y, c = net.s, net.z, net.y, net.c
     rc = buf["rc"]
@@ -220,7 +224,7 @@
     def cores(z1):
         net.recv(rc.at[z1], (tag, "c", z1))
         for y1 in (0, 1):
-            rc[z1, y1] = rc[z1, y1] + part[z1, y1, c]
+            rc[z1, y1] = rc[z1, y1] + own(z1, y1)
         net.send(rc.at[z1, 1 - y, :, :, a_cols], buf["ya"].at[z1], y_dev, (tag, "ya", z1), lambda: buf["ya"].at[z1])
         net.send(rc.at[z1, :, 1 - s, :, b_cols], buf["xb"].at[z1], x_dev, (tag, "xb", z1), lambda: buf["xb"].at[z1])
 
@@ -239,18 +243,20 @@
 
     def wave(k):
         def go(way, z_here, order):
-            na, nb, step = ("da", "db", 1) if way == "up" else ("ua", "ub", -1)
+            step = 1 if way == "up" else -1
             for z1 in order:
+                place = z1 + 1 if way == "up" else z1
+                a_like = lambda place=place: buf["za"].at[place]
+                b_like = lambda place=place: buf["zb"].at[place]
                 if k > 0:
-                    net.recv(buf[na].at[z1], (tag, na, z1))
-                    add_a(z1, buf[na].at[z1])
-                    net.recv(buf[nb].at[z1], (tag, nb, z1))
-                    add_b(z1, buf[nb].at[z1])
+                    net.recv(a_like(), (tag, "za", place))
+                    add_a(z1, a_like())
+                    net.recv(b_like(), (tag, "zb", place))
+                    add_b(z1, b_like())
                 if z1 != z_here:
                     to = net.at(z=z + step)
-                    a_like, b_like = (lambda z1=z1: buf[na].at[z1]), (lambda z1=z1: buf[nb].at[z1])
-                    net.send(rc.at[z1, y, :, :, a_cols], a_like(), to, (tag, na, z1), a_like)
-                    net.send(rc.at[z1, :, s, :, b_cols], b_like(), to, (tag, nb, z1), b_like)
+                    net.send(rc.at[z1, y, :, :, a_cols], a_like(), to, (tag, "za", place), a_like)
+                    net.send(rc.at[z1, :, s, :, b_cols], b_like(), to, (tag, "zb", place), b_like)
 
         net.when(net.here[k], lambda: go("up", k, range(depth - 1, k - 1, -1)))
         net.when(net.here[depth - 1 - k], lambda: go("down", depth - 1 - k, range(0, depth - k)))
@@ -317,122 +323,678 @@
     return [functools.partial(start, 0)] + [functools.partial(finish, k) for k in range(len(partners))]
 
 
-def gather_kernel(attn_own, ffn_own, enc, attn_full, ffn_full, enc_got, send_sems, recv_sems, local_sems):
-    net = Net(send_sems, recv_sems)
+PAIR = 2 * HEAD_DIM
+
+
+def dg(left, right, left_dim, right_dim):
+    return lax.dot_general(
+        left, right, (((left_dim,), (right_dim,)), ((), ())), preferred_element_type=F32
+    )
+
+
+def lane_ids(rows):
+    return lax.broadcasted_iota(jnp.int32, (rows, PAIR), 1)
+
+
+def head_lanes(h):
+    lane = lane_ids(1)
+    return jnp.where((lane >= h * HEAD_DIM) & (lane < (h + 1) * HEAD_DIM), 1.0, 0.0).astype(BF)
+
+
+def spare_lanes(h):
+    lane, first = lane_ids(1), (1 - h) * HEAD_DIM
+    return jnp.where((lane >= first) & (lane < first + 3), 1.0, 0.0).astype(BF)
+
+
+def with_constant(values, constant, h):
+    high = constant.astype(BF).astype(F32)
+    mid = (constant - high).astype(BF).astype(F32)
+    low = constant - high - mid
+    lane, first = lane_ids(values.shape[0]), (1 - h) * HEAD_DIM
+    own = (lane >= h * HEAD_DIM) & (lane < (h + 1) * HEAD_DIM)
+    out = jnp.where(own, values, 0.0)
+    for k, term in enumerate((high, mid, low)):
+        out = jnp.where(lane == first + k, term, out)
+    return out.astype(BF)
+
+
+def pair_lanes(p):
+    return pl.ds(pl.multiple_of(p * PAIR, PAIR), PAIR)
+
+
+def norm_rows(r, gain, shift):
+    mean = jnp.mean(r, axis=-1, keepdims=True)
+    centered = r - mean
+    var = jnp.mean(centered * centered, axis=-1, keepdims=True)
+    inv = lax.rsqrt(var + EPSILON)
+    normed = centered * inv
+    return normed * gain + shift, normed, inv
+
+
+def norm_rows_back(grad, normed, inv, gain):
+    dn = grad * gain
+    out = inv * (
+        dn
+        - jnp.mean(dn, axis=-1, keepdims=True)
+        - normed * jnp.mean(dn * normed, axis=-1, keepdims=True)
+    )
+    return out
+
+
+def rowsum(values):
+    return jnp.sum(values, axis=0, keepdims=True)
+
+
+def by_rows(length, body, step=64):
+    def go(k, carry):
+        body(pl.ds(pl.multiple_of(k * step, step), step))
+        return carry
+
+    lax.fori_loop(0, length // step, go, 0)
+
+
+def allowed_bias(bias, seg_row, seg_col):
+    length = bias.shape[0]
+
+    def body(span):
+        shape = (span.size, length)
+        query = lax.broadcasted_iota(jnp.int32, shape, 0) + span.start
+        key = lax.broadcasted_iota(jnp.int32, shape, 1)
+        ok = (key <= query) & (seg_col[span, :] == seg_row[...])
+        bias[span, :] = jnp.where(ok, 0.0, NEG_FILL)
+
+    by_rows(length, body)
+
+
+def attend_pair(p, q, k, v, q_aug, out, bias):
+    lanes = pair_lanes(p)
+    half = q.shape[0] // 2
+    blocks = [(0, half, k.shape[0]), (half, half, k.shape[0])]
+    if bias is not None:
+        blocks = [(0, half, half), (half, half, 2 * half)]
+    for first, rows, keys in blocks:
+        span = pl.ds(first, rows)
+        q_rows = q[span, lanes]
+        k_rows, v_rows = k[pl.ds(0, keys), lanes], v[pl.ds(0, keys), lanes]
+        outs = []
+        for h in (0, 1):
+            scores = dg(q_rows * head_lanes(h), k_rows, 1, 1)
+            if bias is not None:
+                scores = scores + bias[span, pl.ds(0, keys)]
+            top = jnp.max(scores, axis=-1, keepdims=True)
+            weight = jnp.exp(scores - top)
+            total = jnp.sum(weight, axis=-1, keepdims=True)
+            prob = (weight * (1.0 / total)).astype(BF)
+            outs.append(dg(prob, v_rows, 1, 0))
+            q_aug[2 * p + h, span, :] = with_constant(q_rows.astype(F32), -(top + jnp.log(total)), h)
+        out[span, lanes] = jnp.where(lane_ids(rows) < HEAD_DIM, outs[0], outs[1]).astype(BF)
+
+
+def whole(ref):
+    return ref[...].reshape(-1, ref.shape[-1])
+
+
+class Local:
+    def __init__(self, sems):
+        self.sems, self.count, self.open = sems, 0, []
+
+    def copy(self, src, dst):
+        move = pltpu.make_async_copy(src, dst, self.sems.at[self.count])
+        self.count += 1
+        move.start()
+        return move
+
+    def save(self, src, dst):
+        self.open.append(self.copy(src, dst))
+
+    def drain(self):
+        for move in self.open:
+            move.wait()
+
+
+FWD_SAVED = ("qa", "k", "v", "a", "h1", "n1", "inv1", "qb", "k2", "v2", "a2", "enc", "dr2", "vec")
+
+
+def forward_kernel(names, *refs):
+    r = dict(zip(names, refs))
+    net = Net(r["send_sems"], r["recv_sems"])
     s, z, y, c = net.s, net.z, net.y, net.c
+    small, attn_full, ffn_full = r["small"], r["attn_full"], r["ffn_full"]
+    local = Local(r["local_sems"])
+    depth = net.depth
+    scale = 1.0 / math.sqrt(HEAD_DIM)
+    pairs = r["x"].shape[1] // PAIR
+
+    attn_full[s, z, y, c] = r["attn_own"][...].astype(BF)
+    ffn_full[s, z, y, c] = r["ffn_own"][...].astype(BF)
     net.greet()
-    moves = [
-        pltpu.make_async_copy(own, full.at[s, z, y, c], local_sems.at[k])
-        for k, (own, full) in enumerate(((attn_own, attn_full), (ffn_own, ffn_full)))
-    ]
-    for move in moves:
-        move.start()
-    attn = gather_ticks(net, attn_full, attn_own, "attn", moves[0].wait)
-    ffn = gather_ticks(net, ffn_full, ffn_own, "ffn", moves[1].wait)
-    quarter = enc.shape[0] // 4
-    attn[0]()
-    ffn[0]()
+    attn = gather_ticks(net, attn_full, attn_full.at[s, z, y, c], "attn")
+    ffn = gather_ticks(net, ffn_full, ffn_full.at[s, z, y, c], "ffn")
+    attn.pop(0)()
+    attn.pop(0)()
+    quarter = r["enc_own"].shape[0] // 4
     for k in range(4):
         rows = pl.ds(k * quarter, quarter)
-        net.send(enc.at[rows], enc_got.at[rows], net.at(s=1 - s), ("enc", k), lambda rows=rows: enc_got.at[rows])
-    for one, two in zip(attn[1:], ffn[1:]):
-        one()
-        two()
+        net.send(r["enc_own"].at[rows], r["enc"].at[rows], net.at(s=1 - s), ("enc", k), lambda rows=rows: r["enc"].at[rows])
+    allowed_bias(r["bias"], r["seg_row"], r["seg_col"])
+    attn.pop(0)()
+    attn.pop(0)()
+    ffn.pop(0)()
+    while attn:
+        attn.pop(0)()
+        if len(attn) in (7, 6):
+            ffn.pop(0)()
+
+    def block(k):
+        return whole(attn_full.at[k // depth, k % depth])
+
+    def tick(p, at):
+        if ffn:
+            run_when(p == at, ffn.pop(0))
+
+    def into_heads(dst, left, right, bias, factor):
+        half = left.shape[0] // 2
+        for k in (0, 1):
+            span = pl.ds(k * half, half)
+            value = dg(left[span, :], right, 1, 0)
+            if bias is not None:
+                value = value + bias
+            if factor is not None:
+                value = value * factor
+            dst[span, :] = value.astype(BF)
+
+    t, length = r["t"], r["x"].shape[0]
+    into_heads(r["q"], r["x"], block(0), small[0:1], scale)
+    into_heads(r["k"], r["x"], block(1), None, None)
+    into_heads(r["v"], r["x"], block(2), small[1:2], None)
+    local.save(attn_full, r["attn_out"])
+
+    def self_body(p, carry):
+        attend_pair(p, r["q"], r["k"], r["v"], r["qa"], r["a"], r["bias"])
+        tick(p, 1)
+        tick(p, 3)
+        return carry
+
+    lax.fori_loop(0, pairs, self_body, 0)
+    t[...] = dg(r["a"][...], block(3), 1, 0)
+
+    def norm_one(span):
+        res = r["x"][span, :].astype(F32) + t[span, :] + small[2:3]
+        hidden, normed, inv = norm_rows(res, small[7:8], small[8:9])
+        r["h1f"][span, :] = hidden
+        r["h1"][span, :] = hidden.astype(BF)
+        r["n1"][span, :] = normed
+        r["inv1"][span, :] = jnp.broadcast_to(inv, (span.size, PAIR))
+
+    by_rows(length, norm_one)
+    into_heads(r["q"], r["h1"], block(4), small[3:4], scale)
     for k in range(4):
-        net.recv(enc_got.at[pl.ds(k * quarter, quarter)], ("enc", k))
+        net.recv(r["enc"].at[pl.ds(k * quarter, quarter)], ("enc", k))
+    if ffn:
+        ffn.pop(0)()
+    into_heads(r["k2"], r["enc"], block(5), None, None)
+    into_heads(r["v2"], r["enc"], block(6), small[4:5], None)
+
+    def cross_body(p, carry):
+        attend_pair(p, r["q"], r["k2"], r["v2"], r["qb"], r["a2"], None)
+        for at in range(pairs):
+            tick(p, at)
+        return carry
+
+    for name in ("qa", "k", "v", "a", "h1", "n1", "inv1", "k2", "v2", "enc"):
+        local.save(r[name], r[name + "_out"])
+    lax.fori_loop(0, pairs, cross_body, 0)
+    for name in ("qb", "a2"):
+        local.save(r[name], r[name + "_out"])
+    t[...] = dg(r["a2"][...], block(7), 1, 0)
+
+    def norm_two(span):
+        res = r["h1f"][span, :] + t[span, :] + small[5:6]
+        hidden, normed, inv = norm_rows(res, small[9:10], small[10:11])
+        r["h1f"][span, :] = hidden
+        r["h2"][span, :] = hidden.astype(BF)
+        r["n2"][span, :] = normed
+        r["inv2"][span, :] = jnp.broadcast_to(inv, (span.size, PAIR))
+
+    by_rows(length, norm_two)
+    while ffn:
+        ffn.pop(0)()
+
+    vec, acc = r["vec"], r["h1f"]
+    vec[...] = jnp.zeros_like(vec)
+    root = math.sqrt(0.5)
+    for k in range(depth):
+        t[...] = dg(r["h2"][...], whole(ffn_full.at[0, k]), 1, 1)
+
+        def gelu(span, k=k):
+            u = t[span, :] + small[13 + k : 14 + k]
+            below = 0.5 + 0.5 * lax.erf(u * root)
+            r["g"][k, span, :] = (u * below).astype(BF)
+            r["gp"][k, span, :] = below + u * (jnp.exp(-0.5 * u * u) * (1.0 / math.sqrt(2.0 * math.pi)))
+
+        by_rows(length, gelu)
+        acc[...] += dg(r["g"][k], whole(ffn_full.at[1, k]), 1, 0)
+
+    def norm_three(span):
+        hidden, normed, inv = norm_rows(acc[span, :] + small[6:7], small[11:12], small[12:13])
+        r["out"][span, :] = hidden
+        cot = r["cot"][span, :]
+        dr3 = norm_rows_back(cot, normed, inv, small[11:12])
+        vec[11:12] += rowsum(cot * normed)
+        vec[12:13] += rowsum(cot)
+        acc[span, :] = dr3
+        low = dr3.astype(BF)
+        r["dy"][span, :] = low
+        vec[6:7] += rowsum(low.astype(F32))
+
+    by_rows(length, norm_three)
+    local.save(r["out"], r["layer_out"])
+    slots = r["slots"]
+    held = [None] * slots.shape[0]
+    used = 0
+
+    def put(left, right, dst):
+        nonlocal used
+        slot = used % len(held)
+        used += 1
+        if held[slot] is not None:
+            held[slot].wait()
+        slots[slot] = dg(left, right, 0, 0).astype(BF).reshape(slots.shape[1:])
+        held[slot] = local.copy(slots.at[slot], dst)
+
+    for k in range(depth):
+        put(r["g"][k], r["dy"][...], r["g_ffn"].at[1, k])
+        t[...] = dg(r["dy"][...], whole(ffn_full.at[1, k]), 1, 1)
+
+        def through(span, k=k):
+            du = (t[span, :] * r["gp"][k, span, :]).astype(BF)
+            r["g"][k, span, :] = du
+            vec[13 + k : 14 + k] += rowsum(du.astype(F32))
+
+        by_rows(length, through)
+    for k in range(depth):
+        put(r["g"][k], r["h2"][...], r["g_ffn"].at[0, k])
+        acc[...] += dg(r["g"][k], whole(ffn_full.at[0, k]), 1, 0)
+
+    def norm_two_back(span):
+        grad, normed = acc[span, :], r["n2"][span, :]
+        vec[9:10] += rowsum(grad * normed)
+        vec[10:11] += rowsum(grad)
+        r["dr2"][span, :] = norm_rows_back(grad, normed, r["inv2"][span, 0:1], small[9:10])
+
+    by_rows(length, norm_two_back)
+    for name in ("dr2", "vec"):
+        local.save(r[name], r[name + "_out"])
+    for move in held:
+        move.wait()
+    local.drain()
     net.drain()
 
 
-def gather_call(attn_own, ffn_own, enc):
+def forward_call(x, enc, seg, cot, attn_own, ffn_own, small):
     rows, width = attn_own.shape
     depth = lax.axis_size("dp") // 4
-    full = jax.ShapeDtypeStruct((2, depth, 2, 2, rows, width), BF)
-    anywhere = pl.BlockSpec(memory_space=pl.ANY)
-    inside = pl.BlockSpec(memory_space=pltpu.VMEM)
-    return pl.pallas_call(
-        gather_kernel,
-        out_shape=(full, full, jax.ShapeDtypeStruct(enc.shape, enc.dtype)),
-        in_specs=[inside, inside, anywhere],
-        out_specs=(anywhere, anywhere, anywhere),
+    length, enc_length = x.shape[0], enc.shape[0]
+    heads = width // HEAD_DIM
+    act, enc_act = ((length, width), BF), ((enc_length, width), BF)
+    wide, aug, stack = ((length, width), F32), ((heads, length, PAIR), BF), ((2, depth, 2, 2, rows, width), BF)
+    col = ((length, PAIR), F32)
+    grads = ((2, depth, 2, 2, 2, rows // 2, width), BF)
+    vec = ((-(-small.shape[0] // 8) * 8, width), F32)
+    kept = dict(qa=aug, k=act, v=act, a=act, h1=act, n1=wide, inv1=col, qb=aug, k2=enc_act, v2=enc_act, a2=act, enc=enc_act, dr2=wide, vec=vec)
+    outs = {"layer_out": wide, "attn_out": stack, "g_ffn": grads, **{name + "_out": kept[name] for name in FWD_SAVED}}
+    inner = dict(kept, attn_full=stack, ffn_full=stack, q=act, bias=((length, length), F32), h1f=wide, t=wide, h2=act, n2=wide, inv2=col, g=((depth, length, width), BF), gp=((depth, length, width), F32), out=wide, dy=act, slots=((2, 2, 2, 2, rows // 2, width), BF))
+    inside, anywhere = pl.BlockSpec(memory_space=pltpu.VMEM), pl.BlockSpec(memory_space=pl.ANY)
+    args = dict(x=x, enc_own=enc, seg_row=seg, seg_col=seg.reshape(-1, 1), cot=cot, attn_own=attn_own, ffn_own=ffn_own, small=small)
+    names = (*args, *outs, *inner, "send_sems", "recv_sems", "local_sems")
+    got = pl.pallas_call(
+        functools.partial(forward_kernel, names),
+        out_shape=tuple(jax.ShapeDtypeStruct(*outs[name]) for name in outs),
+        in_specs=[anywhere if name == "enc_own" else inside for name in args],
+        out_specs=(anywhere,) * len(outs),
         scratch_shapes=[
+            *[pltpu.VMEM(*inner[name]) for name in inner],
             pltpu.SemaphoreType.DMA((192,)),
             pltpu.SemaphoreType.DMA((192,)),
-            pltpu.SemaphoreType.DMA((2,)),
+            pltpu.SemaphoreType.DMA((32,)),
         ],
-        compiler_params=pltpu.CompilerParams(collective_id=0, has_side_effects=True),
-        name="gather_all",
-    )(attn_own, ffn_own, enc)
-
-
-NAMES = ("rc", "ya", "xb", "da", "ua", "db", "ub", "xa", "yb", "xc")
-
-
-def reduce_kernel(attn_part, ffn_part, small, attn_out, ffn_out, small_out, send_sems, recv_sems, sums, got, *bufs):
-    net = Net(send_sems, recv_sems)
+        compiler_params=pltpu.CompilerParams(collective_id=0, has_side_effects=True, vmem_limit_bytes=62 << 20),
+        name="gather_and_forward",
+    )(*args.values())
+    return dict(zip(outs, got))
+
+
+def attend_pair_back(p, q_aug, k, v, a, da, dq, dk, dv, bias):
+    lanes = pair_lanes(p)
+    length, keys_all = da.shape[0], k.shape[0]
+    half = length // 2
+    blocks = [(half, half, keys_all), (0, half, keys_all)]
+    if bias is not None:
+        keys_all = length
+        blocks = [(half, half, length), (0, half, half)]
+    sums = None
+    for first, rows, keys in blocks:
+        span = pl.ds(first, rows)
+        k_rows, v_rows = k[pl.ds(0, keys), lanes], v[pl.ds(0, keys), lanes]
+        grad = da[span, lanes]
+        grad_wide = grad.astype(F32)
+        prod = grad_wide * a[span, lanes].astype(F32)
+        q0, q1 = q_aug[2 * p, span, :], q_aug[2 * p + 1, span, :]
+        q_t = (q0 * head_lanes(0) + q1 * head_lanes(1)).T
+        grad_t = grad.T
+        dqs, dks, dvs = [], [], []
+        for h, q_h in ((0, q0), (1, q1)):
+            lane = lane_ids(rows)
+            own = (lane >= h * HEAD_DIM) & (lane < (h + 1) * HEAD_DIM)
+            dot = jnp.sum(jnp.where(own, prod, 0.0), axis=-1, keepdims=True)
+            spare = spare_lanes(h)
+            keep = 1 - spare
+            scores = dg(q_h, k_rows * keep + spare, 1, 1)
+            if bias is not None:
+                scores = scores + bias[span, pl.ds(0, keys)]
+            prob = jnp.exp(scores)
+            d_prob = dg(with_constant(grad_wide, -dot, h), v_rows * keep + spare, 1, 1)
+            d_score = (prob * d_prob).astype(BF)
+            own_rows = slice(h * HEAD_DIM, (h + 1) * HEAD_DIM)
+            dqs.append(dg(d_score, k_rows, 1, 0))
+            dvs.append(dg(grad_t[own_rows], prob.astype(BF), 1, 0))
+            dks.append(dg(q_t[own_rows], d_score, 1, 0))
+        d_q = jnp.where(lane_ids(rows) < HEAD_DIM, dqs[0], dqs[1]).astype(BF)
+        dq[span, lanes] = (d_q.astype(F32) * (1.0 / math.sqrt(HEAD_DIM))).astype(BF)
+        new = [jnp.concatenate(parts, 0) for parts in (dks, dvs)]
+        if sums is None:
+            sums = new
+        else:
+            sums = [
+                old + term if keys == keys_all else jnp.concatenate([old[:, :keys] + term, old[:, keys:]], 1)
+                for old, term in zip(sums, new)
+            ]
+    for ref, value in zip((dk, dv), sums):
+        ref[pl.ds(0, keys_all), lanes] = value.astype(BF).T
+
+
+def backward_kernel(names, *refs):
+    r = dict(zip(names, refs))
+    net = Net(r["send_sems"], r["recv_sems"])
+    s, z, y, c = net.s, net.z, net.y, net.c
+    local = Local(r["local_sems"])
+    depth = net.depth
+    small, vec, stack = r["small"], r["vec"], r["g_attn"]
+    pairs = r["x"].shape[1] // PAIR
+    length = r["x"].shape[0]
     net.greet([to for to in total_partners(net)[2:-1]])
-    count = len(NAMES)
-    plans = []
-    for k, (part, out, side) in enumerate(((ffn_part, ffn_out, 1), (ffn_part, ffn_out, 0), (attn_part, attn_out, 1), (attn_part, attn_out, 0))):
-        buf = dict(zip(NAMES, bufs[k * count : (k + 1) * count]))
-        plans.append(reduce_ticks(net, part.at[side], buf, out, side, k))
-    sums[0] = small[...]
-    total = total_ticks(net, sums, got, "small")
-    for plan in plans:
-        for tick in plan[0]:
-            tick()
-    for plan in plans:
-        for tick in plan[1]:
-            tick()
-    total[0]()
-    total = total[1:]
-    count = len(plans)
-    for t in range(count + 1):
-        if t < count:
-            for tick in plans[t][2]:
-                tick()
-            plans[t][3][0]()
-            plans[t][3][1]()
-        if t > 0:
-            plans[t - 1][3][2]()
-            for tick in plans[t - 1][3][3:-3]:
-                tick()
-            plans[t - 1][3][-3]()
-        if t < len(total):
-            total[t]()
-        if t > 0:
-            plans[t - 1][3][-2]()
-            plans[t - 1][3][-1]()
-    for tick in total[count + 1:]:
-        tick()
-    small_out[...] = sums[sums.shape[0] - 1]
+
+    bufs = [{name: r[name + str(k)] for name in reduce_buffers(1, 2, 2 * CUT)} for k in range(4)]
+    held = [None] * depth
+
+    def load_own(side, z1):
+        held[z1] = local.count
+        local.copy(r["g_ffn"].at[side, z1, :, c], r["own"].at[z1])
+
+    def own_ffn(z1, y1):
+        return r["own"][z1, y1]
+
+    f1 = reduce_ticks(net, r["g_ffn"].at[1], own_ffn, bufs[0], r["ffn_grad"], 1, "f1")
+    f0 = reduce_ticks(net, r["g_ffn"].at[0], own_ffn, bufs[1], r["ffn_grad"], 0, "f0")
+    cross = reduce_ticks(net, stack.at[1], lambda z1, y1: stack[1, z1, y1, c], bufs[2], r["attn_grad"], 1, "cross")
+    self_ = reduce_ticks(net, stack.at[0], lambda z1, y1: stack[0, z1, y1, c], bufs[3], r["attn_grad"], 0, "self")
+
+    loads = {}
+
+    def load(key, src, dst):
+        loads[key] = local.copy(src, dst)
+
+    def load_weight(k, slot):
+        load(("w", k), r["w"].at[k // depth, k % depth], r["slots"].at[slot])
+
+    def weight(k, slot):
+        loads[("w", k)].wait()
+        return whole(r["slots"].at[slot])
+
+    for z1 in range(depth):
+        f1[0][z1]()
+    load("dr2", r["dr2_in"], r["dr2"])
+    load("a2", r["a2_in"], r["a"])
+    load_weight(7, 0)
+    for name in ("qb", "k2", "v2"):
+        load(name, r[name + "_in"], r[name[0] + "s"])
+    load("enc", r["enc_in"], r["enc"])
+    load("h1", r["h1_in"], r["h1"])
+    load_weight(5, 1)
+    load_weight(6, 2)
+    for z1 in range(depth):
+        load_own(1, z1)
+    for z1 in range(depth):
+        f0[0][z1]()
+
+    vec[...] = r["vec_in"][...]
+
+    def cores_ffn(batch, z1, then):
+        like = r["g_ffn"].at[0, z1, :, 0], r["own"].at[z1]
+        pltpu.make_async_copy(*like, local.sems.at[held[z1]]).wait()
+        batch[1][z1]()
+        if then:
+            load_own(0, z1)
+
+    queue = [functools.partial(cores_ffn, f1, z1, True) for z1 in range(depth)]
+    queue += [functools.partial(cores_ffn, f0, z1, False) for z1 in range(depth)]
+
+    def several(*steps):
+        return lambda: [step() for step in steps]
+
+    queue = [several(*queue[:depth]), several(*queue[depth:])]
+    queue += [several(*f1[2], f1[3][0]), f1[3][1], f1[3][2], several(*f0[2], f0[3][0])]
+
+    def tick(p, at):
+        if queue:
+            run_when(p == at, queue.pop(0))
+
+    def put(value, side, z1):
+        stack[side, z1] = value.astype(BF).reshape(stack.shape[2:])
+
+    def colsum(ref):
+        return rowsum(ref.astype(F32))
+
+    def low_dot(dst, left, right):
+        half = left.shape[0] // 2
+        for k in (0, 1):
+            span = pl.ds(k * half, half)
+            dst[span, :] = dg(left[span, :], right, 1, 1).astype(BF)
+
+    def colsum_into(row, ref, rows):
+        vec[row : row + 1] = jnp.zeros_like(vec[row : row + 1])
+
+        def body(span):
+            vec[row : row + 1] += colsum(ref[span, :])
+
+        by_rows(rows, body)
+
+    loads["dr2"].wait()
+
+    def round_dr2(span):
+        r["do"][span, :] = r["dr2"][span, :].astype(BF)
+
+    by_rows(length, round_dr2)
+    colsum_into(5, r["do"], length)
+    loads["a2"].wait()
+    low_dot(r["da"], r["do"], weight(7, 0))
+    put(dg(r["a"][...], r["do"][...], 0, 0), 1, 3)
+    cross[0][3]()
+    load_weight(4, 0)
+    for name in ("qb", "k2", "v2"):
+        loads[name].wait()
+
+    def cross_body(p, carry):
+        for at in range(pairs):
+            tick(p, at)
+        attend_pair_back(p, r["qs"], r["ks"], r["vs"], r["a"], r["da"], r["dq"], r["dk"], r["dv"], None)
+        return carry
+
+    lax.fori_loop(0, pairs, cross_body, 0)
+    load("qa", r["qa_in"], r["qs"])
+    load("k", r["k_in"], r["ks"].at[pl.ds(0, length)])
+    load("v", r["v_in"], r["vs"].at[pl.ds(0, length)])
+    load("a", r["a_in"], r["a"])
+    loads["h1"].wait()
+    loads["enc"].wait()
+    put(dg(r["h1"][...], r["dq"][...], 0, 0), 1, 0)
+    cross[0][0]()
+    put(dg(r["enc"][...], r["dk"][...], 0, 0), 1, 1)
+    cross[0][1]()
+    put(dg(r["enc"][...], r["dv"][...], 0, 0), 1, 2)
+    cross[0][2]()
+    load("n1", r["n1_in"], r["n1"])
+    load("inv1", r["inv1_in"], r["inv1"])
+    from_keys, from_values = weight(5, 1), weight(6, 2)
+    quarter = r["enc"].shape[0] // 4
+    for k in range(4):
+        span = pl.ds(k * quarter, quarter)
+        r["enc"][span, :] = (dg(r["dk"][span, :], from_keys, 1, 1) + dg(r["dv"][span, :], from_values, 1, 1)).astype(BF)
+    for k in range(4):
+        rows = pl.ds(k * quarter, quarter)
+        net.send(r["enc"].at[rows], r["enc_got"].at[rows], net.at(s=1 - s), ("enc", k), lambda rows=rows: r["enc"].at[rows])
+    load_weight(3, 1)
+    colsum_into(3, r["dq"], length)
+    colsum_into(4, r["dv"], r["dv"].shape[0])
+    r["dr2"][...] += dg(r["dq"][...], weight(4, 0), 1, 1)
+    load_weight(0, 2)
+    load_weight(1, 0)
+    for tick_ in cross[1]:
+        tick_()
+    loads["n1"].wait()
+    loads["inv1"].wait()
+    vec[7:8] = jnp.zeros_like(vec[7:8])
+    vec[8:9] = jnp.zeros_like(vec[8:9])
+    vec[2:3] = jnp.zeros_like(vec[2:3])
+
+    def norm_one_back(span):
+        grad, normed = r["dr2"][span, :], r["n1"][span, :]
+        vec[7:8] += rowsum(grad * normed)
+        vec[8:9] += rowsum(grad)
+        grad = norm_rows_back(grad, normed, r["inv1"][span, 0:1], small[7:8])
+        r["dr2"][span, :] = grad
+        low = grad.astype(BF)
+        r["do"][span, :] = low
+        vec[2:3] += rowsum(low.astype(F32))
+
+    by_rows(length, norm_one_back)
+    low_dot(r["da"], r["do"], weight(3, 1))
+    load_weight(2, 1)
+    loads["a"].wait()
+    put(dg(r["a"][...], r["do"][...], 0, 0), 0, 3)
+    self_[0][3]()
+    allowed_bias(r["bias"], r["seg_row"], r["seg_col"])
+    for name in ("qa", "k", "v"):
+        loads[name].wait()
+
+    queue += [f1[3][3], f0[3][1], several(*f1[3][4:]), several(*cross[2], cross[3][0]), f0[3][2]]
+
+    def self_body(p, carry):
+        for at in range(pairs):
+            tick(p, at)
+        attend_pair_back(p, r["qs"], r["ks"], r["vs"], r["a"], r["da"], r["dq"], r["dk"], r["dv"], r["bias"])
+        return carry
+
+    lax.fori_loop(0, pairs, self_body, 0)
+    x = r["x"]
+    near = pl.ds(0, length)
+    put(dg(x[...], r["dq"][...], 0, 0), 0, 0)
+    self_[0][0]()
+    put(dg(x[...], r["dk"][near, :], 0, 0), 0, 1)
+    self_[0][1]()
+    put(dg(x[...], r["dv"][near, :], 0, 0), 0, 2)
+    self_[0][2]()
+    colsum_into(0, r["dq"], length)
+    colsum_into(1, r["dv"], length)
+    r["sums"][0] = vec[...]
+    total = total_ticks(net, r["sums"], r["sum_got"], "small")
+    total.pop(0)()
+    while queue:
+        queue.pop(0)()
+    r["dr2"][...] += dg(r["dq"][...], weight(0, 2), 1, 1)
+    for tick_ in self_[1]:
+        tick_()
+    r["dr2"][...] += dg(r["dk"][near, :], weight(1, 0), 1, 1)
+    cross[3][1]()
+    r["dr2"][...] += dg(r["dv"][near, :], weight(2, 1), 1, 1)
+    local.save(r["dr2"], r["input_grad"])
+    total.pop(0)()
+    f0[3][3]()
+    cross[3][2]()
+    total.pop(0)()
+    for tick_ in f0[3][4:]:
+        tick_()
+    cross[3][3]()
+    for tick_ in self_[2]:
+        tick_()
+    self_[3][0]()
+    total.pop(0)()
+    self_[3][1]()
+    for tick_ in cross[3][4:]:
+        tick_()
+    self_[3][2]()
+    total.pop(0)()
+    for k in range(4):
+        net.recv(r["enc_got"].at[pl.ds(k * quarter, quarter)], ("enc", k))
+
+    for k in (0, 1):
+
+        def widen(span, k=k):
+            r["n1"][span, :] = r["enc_got"][pl.ds(span.start + k * length, span.size), :].astype(F32)
+
+        by_rows(length, widen)
+        local.copy(r["n1"], r["enc_grad"].at[pl.ds(k * length, length)]).wait()
+    while total:
+        total.pop(0)()
+    for tick_ in self_[3][3:]:
+        tick_()
+    r["small_grad"][...] = r["sums"][r["sums"].shape[0] - 1]
+    local.drain()
     net.drain()
 
 
-def reduce_call(attn_part, ffn_part, small):
-    width = attn_part.shape[-1]
+def backward_call(x, seg, small, kept, rows):
+    width = x.shape[1]
+    depth = lax.axis_size("dp") // 4
     devices = lax.axis_size("dp") * 2
-    depth = lax.axis_size("dp") // 4
-    rows = attn_part.shape[0] // devices
-    shape = (2, depth, 2, 2, 2, rows // 2, width)
-    inside = pl.BlockSpec(memory_space=pltpu.VMEM)
-    shapes = reduce_buffers(depth, rows, width)
+    length, enc_length = x.shape[0], kept["enc_out"].shape[0]
+    heads = width // HEAD_DIM
     steps = net_bits(devices)
-    out = jax.ShapeDtypeStruct((2, rows // 2, width), F32)
-    return pl.pallas_call(
-        reduce_kernel,
-        out_shape=(out, out, jax.ShapeDtypeStruct(small.shape, F32)),
-        in_specs=[inside] * 3,
-        out_specs=(inside,) * 3,
+    act, enc_act, wide = ((length, width), BF), ((enc_length, width), BF), ((length, width), F32)
+    own_rows = ((2, rows // 2, width), F32)
+    vec = (kept["vec_out"].shape, F32)
+    outs = dict(input_grad=wide, enc_grad=((enc_length, width), F32), attn_grad=own_rows, ffn_grad=own_rows, small_grad=vec)
+    inner = dict(
+        g_attn=((2, depth, 2, 2, 2, rows // 2, width), BF),
+        own=((depth, 2, 2, rows // 2, width), BF),
+        slots=((3, 2, 2, rows, width), BF),
+        qs=((heads, length, PAIR), BF),
+        ks=enc_act, vs=enc_act, enc=enc_act, enc_got=enc_act, a=act, h1=act, da=act, do=act, dq=act, dk=enc_act, dv=enc_act,
+        dr2=wide, n1=wide, inv1=((length, PAIR), F32), bias=((length, length), F32), vec=vec,
+        sums=((steps + 1, *vec[0]), F32), sum_got=((steps, *vec[0]), F32),
+    )
+    for k in range(4):
+        inner.update({name + str(k): (shape, BF) for name, shape in reduce_buffers(depth, rows, width).items()})
+    inside, anywhere = pl.BlockSpec(memory_space=pltpu.VMEM), pl.BlockSpec(memory_space=pl.ANY)
+    args = dict(x=x, seg_row=seg, seg_col=seg.reshape(-1, 1), small=small, vec_in=kept["vec_out"])
+    far = {name + "_in": kept[name + "_out"] for name in ("dr2", "a2", "qb", "k2", "v2", "enc", "h1", "qa", "k", "v", "a", "n1", "inv1")}
+    far.update(w=kept["attn_out"], g_ffn=kept["g_ffn"])
+    names = (*args, *far, *outs, *inner, "send_sems", "recv_sems", "local_sems")
+    got = pl.pallas_call(
+        functools.partial(backward_kernel, names),
+        out_shape=tuple(jax.ShapeDtypeStruct(*outs[name]) for name in outs),
+        in_specs=[inside] * len(args) + [anywhere] * len(far),
+        out_specs=tuple(anywhere if name in ("input_grad", "enc_grad") else inside for name in outs),
         scratch_shapes=[
+            *[pltpu.VMEM(*inner[name]) for name in inner],
             pltpu.SemaphoreType.DMA((192,)),
             pltpu.SemaphoreType.DMA((192,)),
-            pltpu.VMEM((steps + 1, *small.shape), F32),
-            pltpu.VMEM((steps, *small.shape), F32),
-            *[pltpu.VMEM(shapes[name], BF) for k in range(4) for name in NAMES],
+            pltpu.SemaphoreType.DMA((48,)),
         ],
-        compiler_params=pltpu.CompilerParams(collective_id=1, has_side_effects=True, vmem_limit_bytes=60 << 20),
-        name="reduce_all",
-    )(attn_part.reshape(shape), ffn_part.reshape(shape), small)
+        compiler_params=pltpu.CompilerParams(collective_id=1, has_side_effects=True, vmem_limit_bytes=63 << 20),
+        name="backward_and_sum",
+    )(*args.values(), *far.values())
+    return dict(zip(outs, got))
 
 
 def partner(value, axis, apart):
@@ -669,62 +1231,63 @@
     rate_matrix,
     rate_vector,
 ):
-    own_kernels = attn_master.shape[0] % 32 == 0 and lax.axis_size("dp") % 4 == 0
-    attn_own, ffn_own = attn_master.astype(BF), ffn_master.astype(BF)
-    if own_kernels:
-        attn_full, ffn_full, enc_got = gather_call(attn_own, ffn_own, encoder_out[0])
-        matrices, ffn_all = (full.reshape(-1, attn_own.shape[-1]) for full in (attn_full, ffn_full))
-        partner_enc = enc_got[None]
+    if attn_master.shape[0] % 32 == 0 and lax.axis_size("dp") % 4 == 0 and decoder_in.shape[0] == 1:
+        kept = forward_call(
+            decoder_in[0], encoder_out[0], segment_ids, cotangent[0], attn_master, ffn_master, small_master
+        )
+        got = backward_call(decoder_in[0], segment_ids, small_master, kept, attn_master.shape[0])
+        layer_out, input_grad, encoder_grad = kept["layer_out"][None], got["input_grad"][None], got["enc_grad"][None]
+        attn_grad, ffn_grad = (got[name].reshape(attn_master.shape) for name in ("attn_grad", "ffn_grad"))
+        small_grad = got["small_grad"][: small_master.shape[0]]
     else:
         matrices, ffn_all = (
-            lax.all_gather(own, ("side", "dp"), axis=0, tiled=True) for own in (attn_own, ffn_own)
+            lax.all_gather(attn_master.astype(jnp.bfloat16), ("side", "dp"), axis=0, tiled=True),
+            lax.all_gather(ffn_master.astype(jnp.bfloat16), ("side", "dp"), axis=0, tiled=True),
         )
+        model_width = matrices.shape[1]
+        hidden_units = ffn_all.shape[0] // 2
+        blocks = [
+            matrices[block_index * model_width : (block_index + 1) * model_width]
+            for block_index in range(8)
+        ]
+        w_in = ffn_all[:hidden_units]
+        w_out = ffn_all[hidden_units:]
         partner_enc = partner(encoder_out, "side", 0)
-    model_width = matrices.shape[1]
-    hidden_units = ffn_all.shape[0] // 2
-    blocks = [
-        matrices[block_index * model_width : (block_index + 1) * model_width]
-        for block_index in range(8)
-    ]
-    w_in = ffn_all[:hidden_units]
-    w_out = ffn_all[hidden_units:]
-    mat_grads = [jnp.zeros((model_width, model_width), jnp.float32) for block_index in range(8)]
-    slots = (0, 1, 2, 3, 4, 7)
-    row_index = 0
-    outcome = layer_row(
-        decoder_in[row_index],
-        partner_enc[row_index],
-        segment_ids[row_index],
-        cotangent[row_index],
-        blocks,
-        w_in,
-        w_out,
-        small_master,
-    )
-    result, grad_input, grad_ck, grad_cv, row_mats, grad_w_in, grad_w_out, vec_grad = outcome
-    results = [result]
-    input_grads = [grad_input]
-    key_grads = [grad_ck]
-    value_grads = [grad_cv]
-    for slot_index, slot_grad in zip(slots, row_mats):
-        mat_grads[slot_index] = slot_grad
-    mat_grads[5] = contract_rows(partner_enc[0], key_grads[0])
-    mat_grads[6] = contract_rows(partner_enc[0], value_grads[0])
-    enc_term = contract_cols(key_grads[0], blocks[5]) + contract_cols(value_grads[0], blocks[6])
-    encoder_grad = partner(enc_term.astype(BF)[None], "side", 0).astype(F32)
-    if own_kernels:
-        attn_part = jnp.concatenate([grad.astype(BF) for grad in mat_grads], 0)
-        ffn_part = jnp.concatenate([grad_w_in.astype(BF), grad_w_out.astype(BF)], 0)
-        padded = jnp.pad(vec_grad, ((0, -vec_grad.shape[0] % 8), (0, 0)))
-        attn_grad, ffn_grad, small_grad = reduce_call(attn_part, ffn_part, padded)
-        attn_grad, ffn_grad = attn_grad.reshape(attn_master.shape), ffn_grad.reshape(ffn_master.shape)
-        small_grad = small_grad[: vec_grad.shape[0]]
-    else:
+        mat_grads = [jnp.zeros((model_width, model_width), jnp.float32) for block_index in range(8)]
+        slots = (0, 1, 2, 3, 4, 7)
+        row_index = 0
+        outcome = layer_row(
+            decoder_in[row_index],
+            partner_enc[row_index],
+            segment_ids[row_index],
+            cotangent[row_index],
+            blocks,
+            w_in,
+            w_out,
+            small_master,
+        )
+        result, grad_input, grad_ck, grad_cv, row_mats, grad_w_in, grad_w_out, vec_grad = outcome
+        layer_out = result[None]
+        input_grad = grad_input[None]
+        key_grads = [grad_ck]
+        value_grads = [grad_cv]
+        for slot_index, slot_grad in zip(slots, row_mats):
+            mat_grads[slot_index] = slot_grad
+        returned = partner(jnp.stack([jnp.stack(key_grads), jnp.stack(value_grads)]), "side", 0)
+        row_index = 0
+        own_rows = encoder_out[row_index]
+        mat_grads[5] = contract_rows(own_rows, returned[0, row_index])
+        mat_grads[6] = contract_rows(own_rows, returned[1, row_index])
+        enc_grads = [
+            contract_cols(returned[0, row_index], blocks[5])
+            + contract_cols(returned[1, row_index], blocks[6])
+        ]
+        encoder_grad = jnp.stack(enc_grads)
         attn_total = jnp.concatenate(mat_grads, 0)
         ffn_total = jnp.concatenate([grad_w_in, grad_w_out], 0)
         attn_grad, ffn_grad = (
-            lax.psum_scatter(total, ("side", "dp"), scatter_dimension=0, tiled=True)
-            for total in (attn_total, ffn_total)
+            lax.psum_scatter(attn_total, ("side", "dp"), scatter_dimension=0, tiled=True),
+            lax.psum_scatter(ffn_total, ("side", "dp"), scatter_dimension=0, tiled=True),
         )
         small_grad = lax.psum(vec_grad, ("side", "dp"))
     attn_new, attn_moment_new, attn_average_new = nesterov(
@@ -736,8 +1299,6 @@
     small_new, small_moment_new, small_average_new = nesterov(
         small_master, small_moment, small_average, small_grad, rate_vector
     )
-    layer_out = jnp.stack(results)
-    input_grad = jnp.stack(input_grads)
     return (
         layer_out,
         input_grad,

time: 552 us -> 357 us (0.65)
  matrix products: 191 us -> 0 us
  Pallas kernels: 259 us -> 333 us
  other arithmetic: 64.6 us -> 5.78 us
  local copies, waits for them, and re-layouts: 21 us -> 9.75 us
    dot_general x42 -> x0, matrix products: 191 us -> none  [the longest x10 53.2 us: contract_cols(): lax.dot_general(left_op, right_op, (((1,), (1,)), ((), ())), preferred_el...]
    pallas_call x2, Pallas kernels: 259 us -> 333 us  [the longest x1 183 us: backward_call(): pl.pallas_call(functools.partial(backward_kernel, names), out_shape=tuple...]
    convert_element_type x5 -> x0, other arithmetic: 31.5 us -> none  [the longest x2 24.5 us: attend_backward(): grad_low = grad_scores.astype(jnp.bfloat16)]
    reduce_sum x10 -> x0, other arithmetic: 18.3 us -> none  [the longest x2 13.8 us: attend_forward(): totals = jnp.sum(exp_scores, axis=-1, keepdims=True)]
    slice x3 -> x0, local copies, waits for them, and re-layouts: 10.5 us -> none  [the longest x1 8.47 us: local(): w_out = ffn_all[hidden_units:]]
    concatenate x1 -> x0, other arithmetic: 8.78 us -> none  [local(): ffn_part = jnp.concatenate([grad_w_in.astype(BF), grad_w_out.astype(BF)], 0)]
  transfers between devices with their start and end apart: 1 -> 0, of which waited for: 0 -> 0; matrix products, arithmetic and copies ran while one was open for 17% -> 0% of each run, Pallas kernels for 31% -> 0%
where the time goes in v2:
time: 357 us; the launch traced here: 351 us
  Pallas kernels  333 us (93%)
  local copies, waits for them, and re-layouts  9.75 us (3%)
  other arithmetic  5.78 us (2%)
    pallas_call x1, Pallas kernels, backward_call(): pl.pallas_call(functools.partial(backward_kernel, names), out_shape=tuple...  183 us
    pallas_call x1, Pallas kernels, forward_call(): pl.pallas_call(functools.partial(forward_kernel, names), out_shape=tuple(...  150 us
    unnamed x23, local copies, waits for them, and re-layouts  8.22 us

profile of v2, /device:TPU:0, one launch (start us, length us, event | category | flops | bytes accessed | tf_op | source)
XLA Modules:
  0.0 351.1 jit_solution(11538987128645493080)
XLA Ops:
  0.6 1.5 copy.30.refs_3_.refs_2_
  2.2 149.8 %gather_and_forward.1 = (f32[512,768]{1,0:T(8,128)}, bf16[2,4,2,2,192,768]{5,4,3,2,1,0:T(8,128)(2,1)}, bf16[2,4,2,2,2,96,768]{6,5,4,3,2,1,0:T(8,128)(2,1)}, bf16...) custom-call(bf16[512,768]{1,0:T(8,128)(2,1)} %bitcast.12, ...), custom_call_target="tpu_custom_call" | custom-call | tf_op jit(solution)/shard_map/gather_and_forward/pallas_call | solution.py:650
  152.0 0.0 copy-start.6
  152.0 0.0 copy-start.7
  152.0 0.0 copy-start.8
  152.0 0.0 copy-start.1
  152.0 183.3 %backward_and_sum.1 = (f32[512,768]{1,0:T(8,128)}, f32[1024,768]{1,0:T(8,128)}, f32[2,96,768]{2,1,0:T(8,128)}, f32[2,96,768]{2,1,0:T(8,128)}, f32[24,768]{1,0:T(8,128)}) custom-call(bf16[512,768]{1,0:T(8,128)(2,1)} %bitcast.13, s32[1,512]{1,0:T(1,128)} %refs_1_.1, s32[512,1]{1,0:T(8,128)} %copy.30.refs_3_.refs_2_, f32[17,768]{1,0:T(8,128)} %refs_3_.1, ...), custom_call_target="tpu_custom_call" | custom-call | tf_op jit(solution)/shard_map/backward_and_sum/pallas_call | solution.py:983
  336.0 0.0 copy-done.6
  336.0 0.0 copy-done.7
  336.0 0.0 copy-done.8
  336.0 1.6 add_multiply_fusion.2
  338.3 0.0 copy-done.1
  338.3 0.0 copy-start.4
  338.3 4.2 %add_multiply_fusion = (f32[192,768]{1,0:T(8,128)}, f32[192,768]{1,0:T(8,128)}, f32[192,768]{1,0:T(8,128)}, f32[192,768]{1,0:T(8,128)}, f32[192,768]{1,0:T(8,128)}, /*index=5*/f32[192,768]{1,0:T(8,128)}) fusion(f32[192,768]{1,0:T(8,128)} %param.26, f32[192,768]{1,0:T(8,128)} %refs_6_.1, f32[]{:T(128)S(6)} %copy.37, f32[192,768]{1,0:T(8,128)} %param.23, ...), kind=kLoop, calls=%fused_computation | loop fusion | flops 2359296 | bytes 8257540 | tf_op jit(solution)/shard_map/add | solution.py:1213
  342.4 0.0 copy-done.4
  342.5 0.0 copy-start.5
  342.5 1.1 copy.39
  343.6 0.8 copy-done.5
  344.4 0.0 copy-start
  344.4 1.1 copy.40
  345.6 1.3 copy-done
  346.9 0.0 copy-start.3
  346.9 1.7 copy.41
  348.6 0.0 copy-done.3
  348.6 0.0 copy-start.2
  348.6 0.8 copy.42
  349.4 0.5 copy-done.2
  349.8 0.8 copy.43
Async XLA Ops:
  152.0 184.0 %copy-start.6 = (f32[17,768]{1,0:T(8,128)S(1)}, f32[17,768]{1,0:T(8,128)}, u32[]{:S(2)}) copy-start(f32[17,768]{1,0:T(8,128)} %refs_3_.1) | copy-start | bytes 156676
  152.0 184.0 %copy-start.7 = (f32[17,768]{1,0:T(8,128)S(1)}, f32[17,768]{1,0:T(8,128)}, u32[]{:S(2)}) copy-start(f32[17,768]{1,0:T(8,128)} %param.27) | copy-start | bytes 156676
  152.0 184.0 %copy-start.8 = (f32[17,768]{1,0:T(8,128)S(1)}, f32[17,768]{1,0:T(8,128)}, u32[]{:S(2)}) copy-start(f32[17,768]{1,0:T(8,128)} %param.24) | copy-start | bytes 156676
  152.0 186.2 %copy-start.1 = (f32[192,768]{1,0:T(8,128)S(1)}, f32[192,768]{1,0:T(8,128)}, u32[]{:S(2)}) copy-start(f32[192,768]{1,0:T(8,128)} %refs_5_.1) | copy-start | bytes 1769476
  338.3 4.2 %copy-start.4 = (f32[512,768]{1,0:T(8,128)S(1)}, f32[512,768]{1,0:T(8,128)}, u32[]{:S(2)}) copy-start(f32[512,768]{1,0:T(8,128)} %get-tuple-element.37) | copy-start | bytes 4718596
  342.5 2.0 copy-start.5
  344.4 2.5 copy-start
  346.9 1.7 copy-start.3
  348.6 1.3 copy-start.2
